TPU v7x, 32 devices: a whole 2x2x4 slice. The times are simulated.
32 devices in a mesh: section: 2 (over core), mp: 4 (over z), dp: 4 (over y, x).
Axes of the slice: x: 2, y: 2, z: 4, core: 2. Of those that a mesh axis runs over, the one named last changes fastest.
Arguments:
- tokens: bfloat16 [48, 512, 512], P('dp', 'mp'), may hold values from -6 to 6
- valid: int32 [48], P('dp'), may hold values 0 or 1
- conv_weight: bfloat16 [2, 9, 512, 512], P('section', None, None, 'mp'), may hold values from -0.09375 to 0.09375
- gain_one: float32 [2, 512], P('section'), may hold values from 0.25 to 1.75
- gain_two: float32 [2, 512], P('section'), may hold values from 0.25 to 1.75
- up_weight: bfloat16 [2, 512, 2048], P('section', None, 'mp'), may hold values from -0.25 to 0.25
- down_weight: bfloat16 [2, 2048, 512], P('section', 'mp'), may hold values from -0.125 to 0.125
- cotangent: bfloat16 [48, 512, 512], P('dp', 'mp'), may hold values from -6 to 6
Outputs:
- block_outputs: bfloat16 [2, 48, 512, 512], P('section', 'dp', 'mp')
- input_grads: bfloat16 [2, 48, 512, 512], P('section', 'dp', 'mp')
- conv_grad: float32 [2, 9, 512, 512], P('section', None, None, 'mp')
- gain_one_grad: float32 [2, 512], P('section', 'mp')
- gain_two_grad: float32 [2, 512], P('section', 'mp')
- up_grad: float32 [2, 512, 2048], P('section', None, 'mp')
- down_grad: float32 [2, 2048, 512], P('section', 'mp')
All inputs are finite; a program needn't handle non-finite values. No bound on the sum of `valid` on one device may be relied on, other than what follows from the above.
Results may differ from a plain program's by a relative error of at most 0.02.
Values may be sent and summed in bfloat16 or wider, within the bound.
A program may use at most 256 MiB of HBM per device.

v0:
```python
import jax
import jax.numpy as jnp
from jax import lax
from jax.sharding import PartitionSpec as P

KERNEL = 9
DILATION = 32
MICRO = 6


def passed_along(x, axis, by):
    count = lax.axis_size(axis)
    pairs = [(i, i + by) for i in range(count) if 0 <= i + by < count]
    return lax.ppermute(x, axis, pairs)


def as_sent(x):

    def short(part):
        return part.astype(jnp.bfloat16) if part.dtype == jnp.float32 else part

    return jax.tree.map(short, x)


def normed(values, gain):
    center = values - jnp.mean(values, axis=-1, keepdims=True)
    spread = jnp.mean(center * center, axis=-1, keepdims=True)
    return center * lax.rsqrt(spread + 1e-05) * gain


def forward_block(inputs, weights, conv_w, gain_a, gain_b, up_w, down_w, dilation):
    normed_in = normed(inputs, gain_a).astype(jnp.bfloat16)
    conv_in = lax.all_gather(normed_in, "mp", axis=0, tiled=True)
    length = conv_in.shape[0]
    margin = KERNEL // 2 * DILATION
    padded = jnp.pad(conv_in, ((margin, margin), (0, 0), (0, 0)))
    conv_out = jnp.zeros(conv_in.shape[:2] + (conv_w.shape[2],), jnp.float32)
    for tap in range(KERNEL):
        window = lax.dynamic_slice_in_dim(
            padded, margin + (tap - KERNEL // 2) * dilation, length, 0
        )
        conv_out = conv_out + jnp.einsum(
            "swd,de->swe", window, conv_w[tap], preferred_element_type=jnp.float32
        )
    activated = jax.nn.gelu(conv_out).astype(jnp.bfloat16)
    act_local = lax.all_to_all(activated, "mp", split_axis=0, concat_axis=2, tiled=True)
    middle = inputs + weights * act_local.astype(jnp.float32)
    ffn_local = normed(middle, gain_b).astype(jnp.bfloat16)
    ffn_in = lax.all_gather(ffn_local, "mp", axis=0, tiled=True)
    pre = jnp.einsum("swd,dh->swh", ffn_in, up_w, preferred_element_type=jnp.float32)
    hidden = jax.nn.gelu(pre).astype(jnp.bfloat16)
    branch = lax.psum_scatter(
        jnp.einsum("swh,hd->swd", hidden, down_w, preferred_element_type=jnp.float32).astype(
            jnp.bfloat16
        ),
        "mp",
        scatter_dimension=0,
        tiled=True,
    ).astype(jnp.float32)
    result = middle + weights * branch
    return (result, (conv_in, conv_out, ffn_in, pre, hidden, inputs, middle))


def backward_block(grad_out, kept, weights, conv_w, gain_a, gain_b, up_w, down_w, dilation):
    conv_in, conv_out, ffn_in, pre, hidden, inputs, middle = kept
    seq_local = inputs.shape[0]
    length = conv_in.shape[0]
    margin = KERNEL // 2 * DILATION
    grad_branch = (weights * grad_out).astype(jnp.bfloat16)
    branch_all = lax.all_gather(grad_branch, "mp", axis=0, tiled=True)
    grad_hidden = jnp.einsum("swd,hd->swh", branch_all, down_w, preferred_element_type=jnp.float32)
    _, gelu_pull = jax.vjp(jax.nn.gelu, pre)
    grad_pre = gelu_pull(grad_hidden)[0].astype(jnp.bfloat16)
    down_part = jnp.einsum("swh,swd->hd", hidden, branch_all, preferred_element_type=jnp.float32)
    up_part = jnp.einsum("swd,swh->dh", ffn_in, grad_pre, preferred_element_type=jnp.float32)
    rows = grad_pre
    grad_ffn = lax.psum_scatter(
        jnp.einsum("swh,dh->swd", rows, up_w, preferred_element_type=jnp.float32).astype(
            jnp.bfloat16
        ),
        "mp",
        scatter_dimension=0,
        tiled=True,
    ).astype(jnp.float32)
    _, norm_pull = jax.vjp(normed, middle, gain_b)
    grad_mid_norm, gain_b_part = norm_pull(grad_ffn)
    grad_mid = grad_out + grad_mid_norm
    grad_act = (weights * grad_mid).astype(jnp.bfloat16)
    act_all = lax.all_to_all(grad_act, "mp", split_axis=2, concat_axis=0, tiled=True)
    _, conv_pull = jax.vjp(jax.nn.gelu, conv_out)
    grad_conv = conv_pull(act_all.astype(jnp.float32))[0].astype(jnp.bfloat16)
    padded = jnp.pad(conv_in, ((margin, margin), (0, 0), (0, 0)))
    conv_parts = []
    for tap in range(KERNEL):
        window = lax.dynamic_slice_in_dim(
            padded, margin + (tap - KERNEL // 2) * dilation, length, 0
        )
        conv_parts.append(
            jnp.einsum("swd,swe->de", window, grad_conv, preferred_element_type=jnp.float32)
        )
    conv_part = jnp.stack(conv_parts)
    grad_padded = jnp.pad(grad_conv, ((margin, margin), (0, 0), (0, 0)))
    total = jnp.zeros(
        (lax.axis_size("mp") * seq_local,) + grad_conv.shape[1:2] + (conv_w.shape[1],), jnp.float32
    )
    for tap in range(KERNEL):
        rows = lax.dynamic_slice_in_dim(
            grad_padded, margin - (tap - KERNEL // 2) * dilation, lax.axis_size("mp") * seq_local, 0
        )
        total = total + jnp.einsum(
            "swe,de->swd", rows, conv_w[tap], preferred_element_type=jnp.float32
        )
    grad_normed = lax.psum_scatter(
        total.astype(jnp.bfloat16), "mp", scatter_dimension=0, tiled=True
    ).astype(jnp.float32)
    _, first_pull = jax.vjp(normed, inputs, gain_a)
    grad_in_norm, gain_a_part = first_pull(grad_normed)
    grad_in = grad_mid + grad_in_norm
    return (grad_in, (conv_part, up_part, down_part, gain_a_part, gain_b_part))


def per_device(tokens, valid, conv_weight, gain_one, gain_two, up_weight, down_weight, cotangent):
    section_index = lax.axis_index("section")
    dilation = 1 + (DILATION - 1) * section_index
    win_dev = tokens.shape[0]
    seq_local = tokens.shape[1]
    width = tokens.shape[2]
    part = win_dev // MICRO
    conv_w = conv_weight[0]
    gain_a = gain_one[0]
    gain_b = gain_two[0]
    up_w = up_weight[0]
    down_w = down_weight[0]
    local_shape = (seq_local, part, width)
    recv_act = jnp.zeros(local_shape, jnp.bfloat16)
    recv_grad = jnp.zeros(local_shape, jnp.bfloat16)
    buffers = None
    totals = (
        jnp.zeros(conv_w.shape, jnp.float32),
        jnp.zeros(up_w.shape, jnp.float32),
        jnp.zeros(down_w.shape, jnp.float32),
        jnp.zeros((width,), jnp.float32),
        jnp.zeros((width,), jnp.float32),
    )
    block_out = jnp.zeros(tokens.shape, jnp.bfloat16)
    in_grads = jnp.zeros(tokens.shape, jnp.bfloat16)
    for tick in range(MICRO + 2):
        ahead = tick - section_index
        ahead_ok = (ahead >= 0) & (ahead < MICRO)
        ahead_row = jnp.clip(ahead, 0, MICRO - 1) * part
        fresh = lax.dynamic_slice_in_dim(tokens, ahead_row, part, 0).transpose(1, 0, 2)
        inputs = jnp.where(section_index == 0, fresh, recv_act).astype(jnp.float32)
        weights = lax.dynamic_slice_in_dim(valid, ahead_row, part, 0).astype(jnp.float32)[
            None, :, None
        ]
        result, kept = forward_block(
            inputs, weights, conv_w, gain_a, gain_b, up_w, down_w, dilation
        )
        if buffers is None:
            buffers = [jnp.zeros((3,) + value.shape, value.dtype) for value in kept]
        buffers = [
            lax.dynamic_update_index_in_dim(buffer, value, tick % 3, 0)
            for buffer, value in zip(buffers, kept)
        ]
        result_low = result.astype(jnp.bfloat16)
        old_rows = lax.dynamic_slice_in_dim(block_out, ahead_row, part, 0)
        new_rows = jnp.where(ahead_ok, result_low.transpose(1, 0, 2), old_rows)
        block_out = lax.dynamic_update_slice_in_dim(block_out, new_rows, ahead_row, 0)
        recv_act = passed_along(result_low, "section", 1)
        if tick >= 1:
            behind = tick - 2 + section_index
            behind_ok = (behind >= 0) & (behind < MICRO)
            behind_row = jnp.clip(behind, 0, MICRO - 1) * part
            slot = (tick + 1 + 2 * section_index) % 3
            kept_back = tuple(
                (lax.dynamic_index_in_dim(buffer, slot, 0, keepdims=False) for buffer in buffers)
            )
            upstream = lax.dynamic_slice_in_dim(cotangent, behind_row, part, 0).transpose(1, 0, 2)
            grad_out = jnp.where(section_index == 1, upstream, recv_grad).astype(jnp.float32)
            back_weights = lax.dynamic_slice_in_dim(valid, behind_row, part, 0).astype(jnp.float32)[
                None, :, None
            ]
            grad_in, parts = backward_block(
                grad_out, kept_back, back_weights, conv_w, gain_a, gain_b, up_w, down_w, dilation
            )
            factor = behind_ok.astype(jnp.float32)
            parts = jax.tree.map(lambda value: value * factor, parts)
            parts = jax.tree.map(
                lambda part: part.astype(jnp.float32), lax.psum(as_sent(parts), "dp")
            )
            totals = jax.tree.map(jnp.add, totals, parts)
            grad_low = grad_in.astype(jnp.bfloat16)
            old_grads = lax.dynamic_slice_in_dim(in_grads, behind_row, part, 0)
            new_grads = jnp.where(behind_ok, grad_low.transpose(1, 0, 2), old_grads)
            in_grads = lax.dynamic_update_slice_in_dim(in_grads, new_grads, behind_row, 0)
            recv_grad = passed_along(grad_low, "section", -1)
    conv_total, up_total, down_total, gain_a_total, gain_b_total = totals
    gain_a_share, gain_b_share = (
        lax.psum_scatter(gain_a_total, "mp", scatter_dimension=0, tiled=True),
        lax.psum_scatter(gain_b_total, "mp", scatter_dimension=0, tiled=True),
    )
    return (
        block_out[None],
        in_grads[None],
        conv_total[None],
        gain_a_share[None],
        gain_b_share[None],
        up_total[None],
        down_total[None],
    )


def solution(mesh):
    in_specs = (
        P("dp", "mp", None),
        P("dp"),
        P("section", None, None, "mp"),
        P("section", None),
        P("section", None),
        P("section", None, "mp"),
        P("section", "mp", None),
        P("dp", "mp", None),
    )
    out_specs = (
        P("section", "dp", "mp", None),
        P("section", "dp", "mp", None),
        P("section", None, None, "mp"),
        P("section", "mp"),
        P("section", "mp"),
        P("section", None, "mp"),
        P("section", "mp", None),
    )
    return jax.shard_map(
        per_device, mesh=mesh, in_specs=in_specs, out_specs=out_specs, check_vma=False
    )
```

profile of v0, /device:TPU:0, one launch (start us, length us, event | category | flops | bytes accessed | tf_op | source)
XLA Modules:
  0.0 1954.4 jit_solution(12937462136053079624)
XLA Ops:
  11.5 30.8 %all-gather.24.cloned.1.call-done = bf16[512,2,512]{2,0,1:T(8,128)(2,1)} async-done(((bf16[128,2,512]{2,0,1:T(8,128)(2,1)}), bf16[512,2,512]{2,0,1:T(8,128)(2,1)}) %all-gather.24.cloned.1.call-update) | async-done | bytes 1048592 | tf_op jit(solution)/shard_map/all_gather | solution.py:33
  66.0 27.0 %all-gather.26.cloned.1.call-done = bf16[512,2,512]{2,0,1:T(8,128)(2,1)} async-done(((bf16[128,2,512]{2,0,1:T(8,128)(2,1)}), bf16[512,2,512]{2,0,1:T(8,128)(2,1)}) %all-gather.26.cloned.1.call-update) | async-done | bytes 1048592 | tf_op jit(solution)/shard_map/all_gather | solution.py:49
  98.2 26.7 %reduce-scatter.23.cloned.1.call-done = bf16[128,2,512]{2,0,1:T(8,128)(2,1)} async-done(((bf16[512,2,512]{2,0,1:T(8,128)(2,1)}), bf16[128,2,512]{2,0,1:T(8,128)(2,1)}) %reduce-scatter.23.cloned.1.call-update) | async-done | bytes 262160 | tf_op jit(solution)/shard_map/reduce_scatter | solution.py:52
  132.7 26.9 %all-gather.28.cloned.1.call-done = bf16[512,2,512]{2,0,1:T(8,128)(2,1)} async-done(((bf16[128,2,512]{2,0,1:T(8,128)(2,1)}), bf16[512,2,512]{2,0,1:T(8,128)(2,1)}) %all-gather.28.cloned.1.call-update) | async-done | bytes 1048592 | tf_op jit(solution)/shard_map/all_gather | solution.py:33
  190.7 22.0 %all-gather.30.cloned.1.call-done = bf16[512,2,512]{2,0,1:T(8,128)(2,1)} async-done(((bf16[128,2,512]{2,0,1:T(8,128)(2,1)}), bf16[512,2,512]{2,0,1:T(8,128)(2,1)}) %all-gather.30.cloned.1.call-update) | async-done | bytes 1048592 | tf_op jit(solution)/shard_map/all_gather | solution.py:49
  221.1 24.9 %reduce-scatter.25.cloned.1.call-done = bf16[128,2,512]{2,0,1:T(8,128)(2,1)} async-done(((bf16[512,2,512]{2,0,1:T(8,128)(2,1)}), bf16[128,2,512]{2,0,1:T(8,128)(2,1)}) %reduce-scatter.25.cloned.1.call-update) | async-done | bytes 262160 | tf_op jit(solution)/shard_map/reduce_scatter | solution.py:52
  256.4 17.8 all-gather.56.cloned.1.call-done
  280.9 22.4 %all-gather.32.cloned.1.call-done = bf16[512,2,512]{2,0,1:T(8,128)(2,1)} async-done(((bf16[128,2,512]{2,0,1:T(8,128)(2,1)}), bf16[512,2,512]{2,0,1:T(8,128)(2,1)}) %all-gather.32.cloned.1.call-update) | async-done | bytes 1048592 | tf_op jit(solution)/shard_map/all_gather | solution.py:33
  370.1 14.4 all-gather.34.cloned.1.call-done
  421.5 24.9 %reduce-scatter.41.cloned.1.call-done = bf16[128,2,512]{2,0,1:T(8,128)(2,1)} async-done(((bf16[512,2,512]{2,0,1:T(8,128)(2,1)}), bf16[128,2,512]{2,0,1:T(8,128)(2,1)}) %reduce-scatter.41.cloned.1.call-update) | async-done | bytes 262160 | tf_op jit(solution)/shard_map/reduce_scatter | solution.py:113
  484.9 25.3 %all-gather.58.cloned.1.call-done = bf16[512,2,512]{2,0,1:T(8,128)(2,1)} async-done(((bf16[128,2,512]{2,0,1:T(8,128)(2,1)}), bf16[512,2,512]{2,0,1:T(8,128)(2,1)}) %all-gather.58.cloned.1.call-update) | async-done | bytes 1048592 | tf_op jit(solution)/shard_map/all_gather | solution.py:70
  527.2 13.0 all-to-all-done.3
  632.0 24.4 %reduce-scatter.45.cloned.1.call-done = bf16[128,2,512]{2,0,1:T(8,128)(2,1)} async-done(((bf16[512,2,512]{2,0,1:T(8,128)(2,1)}), bf16[128,2,512]{2,0,1:T(8,128)(2,1)}) %reduce-scatter.45.cloned.1.call-update) | async-done | bytes 262160 | tf_op jit(solution)/shard_map/reduce_scatter | solution.py:113
  695.0 25.3 %all-gather.60.cloned.1.call-done = bf16[512,2,512]{2,0,1:T(8,128)(2,1)} async-done(((bf16[128,2,512]{2,0,1:T(8,128)(2,1)}), bf16[512,2,512]{2,0,1:T(8,128)(2,1)}) %all-gather.60.cloned.1.call-update) | async-done | bytes 1048592 | tf_op jit(solution)/shard_map/all_gather | solution.py:70
  737.1 13.1 all-to-all-done.4
  841.2 25.1 %reduce-scatter.49.cloned.1.call-done = bf16[128,2,512]{2,0,1:T(8,128)(2,1)} async-done(((bf16[512,2,512]{2,0,1:T(8,128)(2,1)}), bf16[128,2,512]{2,0,1:T(8,128)(2,1)}) %reduce-scatter.49.cloned.1.call-update) | async-done | bytes 262160 | tf_op jit(solution)/shard_map/reduce_scatter | solution.py:113
  904.7 25.3 %all-gather.62.cloned.1.call-done = bf16[512,2,512]{2,0,1:T(8,128)(2,1)} async-done(((bf16[128,2,512]{2,0,1:T(8,128)(2,1)}), bf16[512,2,512]{2,0,1:T(8,128)(2,1)}) %all-gather.62.cloned.1.call-update) | async-done | bytes 1048592 | tf_op jit(solution)/shard_map/all_gather | solution.py:70
  1049.1 25.1 %reduce-scatter.53.cloned.1.call-done = bf16[128,2,512]{2,0,1:T(8,128)(2,1)} async-done(((bf16[512,2,512]{2,0,1:T(8,128)(2,1)}), bf16[128,2,512]{2,0,1:T(8,128)(2,1)}) %reduce-scatter.53.cloned.1.call-update) | async-done | bytes 262160 | tf_op jit(solution)/shard_map/reduce_scatter | solution.py:113
  1112.7 25.4 %all-gather.64.cloned.1.call-done = bf16[512,2,512]{2,0,1:T(8,128)(2,1)} async-done(((bf16[128,2,512]{2,0,1:T(8,128)(2,1)}), bf16[512,2,512]{2,0,1:T(8,128)(2,1)}) %all-gather.64.cloned.1.call-update) | async-done | bytes 1048592 | tf_op jit(solution)/shard_map/all_gather | solution.py:70
  1256.4 25.0 %reduce-scatter.57.cloned.1.call-done = bf16[128,2,512]{2,0,1:T(8,128)(2,1)} async-done(((bf16[512,2,512]{2,0,1:T(8,128)(2,1)}), bf16[128,2,512]{2,0,1:T(8,128)(2,1)}) %reduce-scatter.57.cloned.1.call-update) | async-done | bytes 262160 | tf_op jit(solution)/shard_map/reduce_scatter | solution.py:113
  1320.4 24.1 %all-gather.66.cloned.1.call-done = bf16[512,2,512]{2,0,1:T(8,128)(2,1)} async-done(((bf16[128,2,512]{2,0,1:T(8,128)(2,1)}), bf16[512,2,512]{2,0,1:T(8,128)(2,1)}) %all-gather.66.cloned.1.call-update) | async-done | bytes 1048592 | tf_op jit(solution)/shard_map/all_gather | solution.py:70
  1496.2 25.7 %all-gather.68.cloned.1.call-done = bf16[512,2,512]{2,0,1:T(8,128)(2,1)} async-done(((bf16[128,2,512]{2,0,1:T(8,128)(2,1)}), bf16[512,2,512]{2,0,1:T(8,128)(2,1)}) %all-gather.68.cloned.1.call-update) | async-done | bytes 1048592 | tf_op jit(solution)/shard_map/all_gather | solution.py:70
  1631.2 16.4 all-reduce.32
  1660.7 276.7 %all-reduce.36.cloned.1.call-done = (bf16[9,512,128]{2,1,0:T(8,128)(2,1)}, bf16[9,512,128]{2,1,0:T(8,128)(2,1)}, bf16[9,512,128]{2,1,0:T(8,128)(2,1)}, bf16[9,51...) async-done(((bf16[9,512,128]{2,1,0:T(8,128)(2,1)}, ...) | async-done | bytes 15597584 | tf_op jit(solution)/shard_map/psum | solution.py:189
  (1288 shorter events, 1127.6 us)
Async XLA Ops:
  98.1 61.5 %all-gather.28.cloned.1.call-start = ((), (), s32[]{:S(2)}) async-start(), calls=%async_computation.40 | async-start | bytes 1310720 | tf_op jit(solution)/shard_map/all_gather | solution.py:33
  221.1 82.2 %all-gather.32.cloned.1.call-start = ((), (), s32[]{:S(2)}) async-start(), calls=%async_computation.43 | async-start | bytes 1310720 | tf_op jit(solution)/shard_map/all_gather | solution.py:33
  256.2 85.7 %reduce-scatter.39.cloned.1.call-start = ((), (), s32[]{:S(2)}) async-start(), calls=%async_computation.62 | async-start | bytes 1310720 | tf_op jit(solution)/shard_map/reduce_scatter | solution.py:77
  355.1 62.7 %reduce-scatter.27.cloned.1.call-start = ((), (), s32[]{:S(2)}) async-start(), calls=%async_computation.45 | async-start | bytes 1310720 | tf_op jit(solution)/shard_map/reduce_scatter | solution.py:52
  396.9 83.8 %all-gather.36.cloned.1.call-start = ((), (), s32[]{:S(2)}) async-start(), calls=%async_computation.46 | async-start | bytes 1310720 | tf_op jit(solution)/shard_map/all_gather | solution.py:33
  468.7 79.2 %reduce-scatter.43.cloned.1.call-start = ((), (), s32[]{:S(2)}) async-start(), calls=%async_computation.65 | async-start | bytes 1310720 | tf_op jit(solution)/shard_map/reduce_scatter | solution.py:77
  565.1 63.4 %reduce-scatter.29.cloned.1.call-start = ((), (), s32[]{:S(2)}) async-start(), calls=%async_computation.48 | async-start | bytes 1310720 | tf_op jit(solution)/shard_map/reduce_scatter | solution.py:52
  607.0 83.8 %all-gather.40.cloned.1.call-start = ((), (), s32[]{:S(2)}) async-start(), calls=%async_computation.49 | async-start | bytes 1310720 | tf_op jit(solution)/shard_map/all_gather | solution.py:33
  677.7 80.2 %reduce-scatter.47.cloned.1.call-start = ((), (), s32[]{:S(2)}) async-start(), calls=%async_computation.68 | async-start | bytes 1310720 | tf_op jit(solution)/shard_map/reduce_scatter | solution.py:77
  774.9 62.7 %reduce-scatter.31.cloned.1.call-start = ((), (), s32[]{:S(2)}) async-start(), calls=%async_computation.51 | async-start | bytes 1310720 | tf_op jit(solution)/shard_map/reduce_scatter | solution.py:52
  816.8 83.7 %all-gather.44.cloned.1.call-start = ((), (), s32[]{:S(2)}) async-start(), calls=%async_computation.52 | async-start | bytes 1310720 | tf_op jit(solution)/shard_map/all_gather | solution.py:33
  889.9 77.8 %reduce-scatter.51.cloned.1.call-start = ((), (), s32[]{:S(2)}) async-start(), calls=%async_computation.71 | async-start | bytes 1310720 | tf_op jit(solution)/shard_map/reduce_scatter | solution.py:77
  982.8 62.7 %reduce-scatter.33.cloned.1.call-start = ((), (), s32[]{:S(2)}) async-start(), calls=%async_computation.54 | async-start | bytes 1310720 | tf_op jit(solution)/shard_map/reduce_scatter | solution.py:52
  1024.8 83.7 %all-gather.48.cloned.1.call-start = ((), (), s32[]{:S(2)}) async-start(), calls=%async_computation.55 | async-start | bytes 1310720 | tf_op jit(solution)/shard_map/all_gather | solution.py:33
  1095.3 80.5 %reduce-scatter.55.cloned.1.call-start = ((), (), s32[]{:S(2)}) async-start(), calls=%async_computation.74 | async-start | bytes 1310720 | tf_op jit(solution)/shard_map/reduce_scatter | solution.py:77
  1190.3 62.7 %reduce-scatter.35.cloned.1.call-start = ((), (), s32[]{:S(2)}) async-start(), calls=%async_computation.57 | async-start | bytes 1310720 | tf_op jit(solution)/shard_map/reduce_scatter | solution.py:52
  1232.0 83.4 %all-gather.52.cloned.1.call-start = ((), (), s32[]{:S(2)}) async-start(), calls=%async_computation.58 | async-start | bytes 1310720 | tf_op jit(solution)/shard_map/all_gather | solution.py:33
  1303.7 84.0 %reduce-scatter.59.cloned.1.call-start = ((), (), s32[]{:S(2)}) async-start(), calls=%async_computation.77 | async-start | bytes 1310720 | tf_op jit(solution)/shard_map/reduce_scatter | solution.py:77
  1397.8 66.2 %reduce-scatter.61.cloned.1.call-start = ((), (), s32[]{:S(2)}) async-start(), calls=%async_computation.78 | async-start | bytes 1310720 | tf_op jit(solution)/shard_map/reduce_scatter | solution.py:113
  1457.3 64.6 %all-gather.68.cloned.1.call-start = ((), (), s32[]{:S(2)}) async-start(), calls=%async_computation.79 | async-start | bytes 1310720 | tf_op jit(solution)/shard_map/all_gather | solution.py:70
  1477.5 77.8 %reduce-scatter.63.cloned.1.call-start = ((), (), s32[]{:S(2)}) async-start(), calls=%async_computation.80 | async-start | bytes 1310720 | tf_op jit(solution)/shard_map/reduce_scatter | solution.py:77
  1528.6 93.8 %reduce-scatter.37.cloned.1.call-start = ((), (), s32[]{:S(2)}) async-start(), calls=%async_computation.60 | async-start | bytes 1310720 | tf_op jit(solution)/shard_map/reduce_scatter | solution.py:52
  1566.2 62.2 %reduce-scatter.65.cloned.1.call-start = ((), (), s32[]{:S(2)}) async-start(), calls=%async_computation.81 | async-start | bytes 1310720 | tf_op jit(solution)/shard_map/reduce_scatter | solution.py:113
  1601.8 335.6 %all-reduce.36.cloned.1.call-start = ((), (), s32[]{:S(2)}) async-start(), calls=%async_computation.82 | async-start | bytes 31195136 | tf_op jit(solution)/shard_map/psum | solution.py:189
  (310 other events, 3148.8 us)
Sparse Core Ops, SparseCore 0:
  11.6 30.6 all-gather.23
  66.0 26.8 all-gather.25
  132.8 26.7 all-gather.27
  185.7 26.9 all-gather.29
  275.8 27.4 all-gather.31
  306.2 30.8 reduce-scatter.38
  355.2 29.2 all-gather.33
  482.8 27.4 all-gather.57
  517.0 30.8 reduce-scatter.42
  565.2 29.2 all-gather.37
  692.8 27.4 all-gather.59
  727.0 30.8 reduce-scatter.46
  775.1 29.2 all-gather.41
  902.6 27.4 all-gather.61
  936.8 30.8 reduce-scatter.50
  983.0 29.2 all-gather.45
  1110.6 27.4 all-gather.63
  1144.9 30.8 reduce-scatter.54
  1190.4 29.2 all-gather.49
  1317.1 27.4 all-gather.65
  1351.3 30.8 reduce-scatter.58
  1494.5 27.4 all-gather.67
  1558.2 30.0 reduce-scatter.36
  1634.6 302.6 all-reduce.35
  (22 shorter events, 579.5 us)
where the time goes:
time: 1970 us; the launch traced here: 1950 us
  waiting for transfers between devices  1010 us (51%)
  matrix products  367 us (19%)
  other arithmetic  250 us (13%)
  local copies, waits for them, and re-layouts  202 us (10%)
  starting transfers between devices  81.2 us (4%)
  blocking collectives  25.7 us (1%)
    psum x1, waiting for transfers between devices, per_device(): lax.psum(as_sent(parts), 'dp')  277 us
    all_gather x7, waiting for transfers between devices, backward_block(): branch_all = lax.all_gather(grad_branch, 'mp', axis=0, tiled=True)  169 us
    reduce_scatter x7, waiting for transfers between devices, backward_block(): lax.psum_scatter(total.astype(jnp.bfloat16), 'mp', scatter_dimension=0, t...  135 us
    all_gather x8, waiting for transfers between devices, forward_block(): conv_in = lax.all_gather(normed_in, 'mp', axis=0, tiled=True)  132 us
    dot_general x63, matrix products, backward_block(): jnp.einsum('swd,swe->de', window, grad_conv, preferred_element_type=jnp.f...  113 us
    all_gather x8, waiting for transfers between devices, forward_block(): ffn_in = lax.all_gather(ffn_local, 'mp', axis=0, tiled=True)  102 us
    all_to_all x8, waiting for transfers between devices, forward_block(): lax.all_to_all(activated, 'mp', split_axis=0, concat_axis=2, tiled=True)  84.9 us
    dot_general x63, matrix products, backward_block(): jnp.einsum('swe,de->swd', rows, conv_w[tap], preferred_element_type=jnp.f...  78.6 us
  transfers between devices with their start and end apart: 74, of which 58 were waited for; matrix products, arithmetic and copies ran while one was open for 28% of the time, Pallas kernels for 0%

commit v1 on v0

v1 whole, which is shorter than its diff:
```python
import jax
import jax.numpy as jnp
from jax import lax
from jax.experimental import pallas as pl
from jax.experimental.pallas import tpu as pltpu
from jax.sharding import PartitionSpec as P

KERNEL = 9
DILATION = 32
HALF = KERNEL // 2
PHASES = 8
TILE = 16
COLS = 256
C0 = 0.7978845608028654
C1 = 0.044715
BF = jnp.bfloat16
F32 = jnp.float32
MESH = pl.DeviceIdType.MESH
LATENCY = 2.0
NEVER = 1e9
AHEAD = 1.0
Z_FIRST = (7,)


def gelu_and_slope(v):
    v2 = v * v
    t = jnp.tanh(v * (C0 + (C0 * C1) * v2))
    h = 0.5 + 0.5 * t
    slope = h + v * (1.0 - t * t) * (0.5 * C0 + (1.5 * C0 * C1) * v2)
    return v * h, slope


def norm_parts(values):
    center = values - jnp.mean(values, axis=-1, keepdims=True)
    r = lax.rsqrt(jnp.mean(center * center, axis=-1, keepdims=True) + 1e-05)
    return center * r, r


def norm_back(g, hat, r):
    return r * (
        g
        - jnp.mean(g, axis=-1, keepdims=True)
        - hat * jnp.mean(g * hat, axis=-1, keepdims=True)
    )


def dot(a, b):
    return jnp.dot(a, b, preferred_element_type=F32)


def dot_nt(a, b):
    return lax.dot_general(a, b, (((1,), (1,)), ((), ())), preferred_element_type=F32)


def make_kernel(mp, dp, nw, seq, width):
    levels = dp.bit_length() - 1
    assert dp == 1 << levels and 2 <= levels <= 4
    rows_all = nw * seq
    q_count = seq // PHASES
    group_rows = width // mp
    half_rows = group_rows // 2
    nblk = KERNEL + 2 * mp
    margin = HALF * DILATION
    conv_groups = [(0, 3), (3, 3), (6, 3)]
    wgroups = [(b, g) for b in range(2) for g in conv_groups + [(KERNEL, mp), (KERNEL + mp, mp)]]
    back_groups = [(0, 3), (3, 3), (6, 2), (8, 1)]
    ggroups = [(b, g) for b in (1, 0) for g in [(KERNEL + mp, mp), (KERNEL, mp)] + back_groups]
    per_grad = len(back_groups) + 2
    z_order = list(Z_FIRST)
    assert len(z_order) <= 2
    z_first = {g: i % 2 for i, g in enumerate(z_order)}
    batches = 3 if nw % 3 == 0 else 1
    wb = nw // batches
    nwg, ngg = len(wgroups), len(ggroups)
    per_block = len(conv_groups) + 2
    piece_cols = width if levels == 2 else width >> (levels - 2)

    def body(tok, cot, valid, one_in, two_in, conv_in, up_in, down_in,
             blk, ing, fin, gout_sum, sp_hid, sp_slo,
             big, recv_c, recv_z, recv_zf, piece, xext, xpad, gpad, hid, slo, x0, x1, x2, midb, ffn,
             slope1, gout, gb, tra, trb, acc, mid, ig1, gains, slab, edge, hsend, hrecv,
             gbuf, grecv, *rest):
        recv_x = rest[:levels]
        (agz_s, agz_r, agf_s, agx_s, agx_r, agk_s, agk_r, own_l, own_s, own_r, rc_s, rc_r, rx_s, rx_r,
         rz_s, rz_r, zf_s, zf_r, rf_s, rf_r, gn_s, gn_r, halo_s, halo_r, out_s, out_r, loc, credit) = rest[levels:]
        s = lax.axis_index("section")
        m = lax.axis_index("mp")
        d = lax.axis_index("dp")

        def dev(ss, mm, dd):
            return {"section": ss, "mp": mm, "dp": dd}

        sibling = dev(1 - s, m, d)

        flipped = 0
        for j in range(levels):
            flipped = flipped + ((d // (1 << j)) % 2) * (1 << (levels - 1 - j))
        place = (1 - s) * d + s * flipped

        def bit(j):
            return (place // (1 << j)) % 2

        def partner(j):
            other = (1 - s) * (1 << j) + s * (1 << (levels - 1 - j))
            has = (d // other) % 2
            return dev(s, m, d + other - 2 * other * has)

        def peer(k):
            return lax.rem(m + k, mp)

        def rcopy(src, dst, ssem, rsem, device):
            return pltpu.make_async_remote_copy(
                src_ref=src, dst_ref=dst, send_sem=ssem, recv_sem=rsem,
                device_id=device, device_id_type=MESH)

        sends = []

        def begin(copy, cond=None, kind=None):
            if cond is None:
                copy.start()
            else:
                pl.when(cond)(copy.start)
            sends.append((copy, cond, kind))

        def flush(kind=None):
            for copy, cond, its in [x for x in sends if kind is None or x[2] == kind]:
                if cond is None:
                    copy.wait_send()
                else:
                    pl.when(cond)(copy.wait_send)
            sends[:] = [x for x in sends if kind is not None and x[2] != kind]

        barrier = pltpu.get_barrier_semaphore()
        count = 0
        for o in range(dp):
            for ss in range(2):
                if o == 0 and ss == 0:
                    continue
                other = d + o - dp * ((d + o) // dp)
                pl.semaphore_signal(
                    barrier, inc=1, device_id=dev(s + ss - 2 * s * ss, m, other), device_id_type=MESH)
                count += 1
        for k in range(1, mp):
            for ss in range(2):
                pl.semaphore_signal(
                    barrier, inc=1, device_id=dev(s + ss - 2 * s * ss, peer(k), d), device_id_type=MESH)
                count += 1
        loads = [
            pltpu.make_async_copy(tok.at[pl.ds(s * nw, nw)], x1, loc.at[0]),
            pltpu.make_async_copy(one_in, gains.at[s, 0], loc.at[1]),
            pltpu.make_async_copy(two_in, gains.at[s, 1], loc.at[2]),
            pltpu.make_async_copy(cot.at[pl.ds(s * nw, nw)], gout, loc.at[3]),
        ]
        for copy in loads:
            copy.start()
        pl.semaphore_wait(barrier, count)

        def shard_view(b, group, mm):
            j0, nj = group
            if j0 < KERNEL:
                return big.at[b, pl.ds(j0, nj), :, :, pl.ds(pl.multiple_of(mm * group_rows, group_rows), group_rows)]
            return big.at[b, j0 + mm]

        def own_source(group):
            j0, nj = group
            if j0 < KERNEL:
                return conv_in.at[pl.ds(j0, nj)]
            return up_in if j0 == KERNEL else down_in

        def sub(ref, half, at, level):
            lead = ref.shape[:-3]
            idx = (slice(None),) * len(lead)
            step = half_rows // min(dp, 4)
            if levels == 2:
                first = ((at // (1 << level)) * (1 << level)) * step
                return ref.at[idx + (slice(None), pl.ds(pl.multiple_of(half * half_rows + first, TILE), step << level))]
            low, high = at % 4, at // 4
            if level <= 2:
                first = ((low // (1 << level)) * (1 << level)) * step
                return ref.at[idx + (pl.ds(high, 1), pl.ds(pl.multiple_of(half * half_rows + first, TILE), step << level))]
            up = level - 2
            first = (high // (1 << up)) * (1 << up)
            return ref.at[idx + (pl.ds(first, 1 << up), pl.ds(pl.multiple_of(half * half_rows, TILE), half_rows))]

        def place_of(half):
            return d if half == 0 else flipped

        own = []
        for i, group in enumerate(conv_groups + [(KERNEL, mp), (KERNEL + mp, mp)]):
            src, dst = own_source(group), shard_view(s, group, m)
            local = pltpu.make_async_copy(src, dst, own_l.at[i])
            local.start()
            own.append(local)
        begin(rcopy(one_in, gains.at[s, 0], gn_s.at[0], gn_r.at[0], sibling))
        begin(rcopy(two_in, gains.at[s, 1], gn_s.at[levels + mp], gn_r.at[levels + mp], sibling))

        def z_copies(n):
            b, group = wgroups[n]
            i = n % per_block
            out = [(rcopy(own_source(group), shard_view(b, group, m), own_s.at[i], own_r.at[i], sibling), None)]
            for k in (2, 1, 3):
                for half in range(2):
                    copy = rcopy(
                        sub(own_source(group), half, place_of(half), 0),
                        sub(shard_view(b, group, m), half, place_of(half), 0),
                        agz_s.at[i, k - 1, half], agz_r.at[n, k - 1], dev(half, peer(k), d))
                    out.append((copy, None if k == 2 else (m != 3 if k == 1 else m != 0)))
            return out

        def z_send(n):
            @pl.when(s == wgroups[n][0])
            def _():
                for copy, cond in z_copies(n):
                    if cond is None:
                        copy.start()
                    else:
                        pl.when(cond)(copy.start)

        def z_flush(n):
            @pl.when(s == wgroups[n][0])
            def _():
                for copy, cond in z_copies(n):
                    if cond is None:
                        copy.wait_send()
                    else:
                        pl.when(cond)(copy.wait_send)

        def received(dst, rsem):
            rcopy(dst, dst, rsem, rsem, sibling).wait_recv()

        def z_forward(n):
            b, group = wgroups[n]
            held = sub(shard_view(b, group, peer(mp - 2)), s, place, 0)
            received(held, agz_r.at[n, 1])
            for at, to, k in ((2, 3, 3), (1, 0, 1)):
                begin(rcopy(held, held, agf_s.at[n], agz_r.at[n, k - 1], dev(s, to, d)), m == at, ("gather", b))

        def run_view(b, group, first, count):
            j0, nj = group
            if j0 < KERNEL:
                return big.at[b, pl.ds(j0, nj), :, :, pl.ds(first * group_rows, count * group_rows)]
            return big.at[b, pl.ds(j0 + first, count)]

        def foreign(n, half, at, level):
            b, group = wgroups[n]
            return sub(run_view(b, group, 0, mp - 1), half, at, level)

        def x_step(n, level):
            b, group = wgroups[n]
            if level == 0:
                for k in (1, 3):
                    received(sub(shard_view(b, group, peer(mp - k)), s, place, 0), agz_r.at[n, k - 1])
            else:
                received(foreign(n, s, place, level - 1), agx_r.at[n, level - 1])
            if level < levels:
                sems, to = (agx_s.at[n, level], agx_r.at[n, level]), partner(level)
            else:
                sems, to = (agk_s.at[n], agk_r.at[n]), sibling
            for mine in range(mp):
                @pl.when(m == mine)
                def _():
                    for first, count in ((0, mine), (mine + 1, mp - 1 - mine)):
                        if count:
                            part = sub(run_view(b, group, first, count), s, place, level)
                            rcopy(part, part, *sems, to).start()
            held = foreign(n, s, place, level)
            sends.append((rcopy(held, held, *sems, to), None, ("gather", b)))

        def gathered(n):
            b, group = wgroups[n]
            i = n % per_block

            @pl.when(s == b)
            def _():
                pltpu.make_async_copy(own_source(group), shard_view(b, group, m), own_l.at[i]).wait()

            @pl.when(s != b)
            def _():
                received(shard_view(b, group, m), own_r.at[i])

            received(foreign(n, 1 - s, 0, levels), agk_r.at[n])

        clock = {"now": 4.0}
        gate = {"open": False}
        busy = {}
        chains = {}

        def post(link, size, rate):
            start = max(clock["now"], busy.get(link, 0.0))
            busy[link] = start + size / rate
            return busy[link] + LATENCY

        def resume(key):
            try:
                chains[key][0] = next(chains[key][1])
            except StopIteration:
                del chains[key]

        def launch(key, chain):
            chains[key] = [0.0, chain]
            resume(key)

        def service():
            while True:
                ready = [(c[0], key) for key, c in chains.items()
                         if c[0] <= clock["now"] + (AHEAD if key[0] == 0 and key[1] < per_block else 0.0)]
                if not ready:
                    return
                when, key = min(ready)
                clock["now"] = max(clock["now"], when)
                resume(key)

        def complete(keys):
            while any(key in chains for key in keys):
                when, key = min((c[0], key) for key, c in chains.items())
                clock["now"] = max(clock["now"], when)
                resume(key)

        def work(cost, call, *args):
            call(*args)
            clock["now"] += cost
            service()

        def gather_chain(n):
            b, group = wgroups[n]
            unit = (group[1] * width * group_rows if group[0] < KERNEL else width * width) * 2 / (2 * dp) / 1e3
            yield post("z", 6 * unit, 100)
            if n == per_block - 2:
                for later in range(per_block, nwg):
                    begin_gather(later)
            if b == 1 and not gate["open"]:
                yield NEVER
            z_forward(n)
            yield clock["now"] + LATENCY
            x_step(n, 0)
            when = post("xy", 3 * unit, 100)
            for level in range(1, levels):
                yield when
                x_step(n, level)
                when = post("xy", 3 * unit * (1 << level), 100)
            if n == per_block - 1:
                gate["open"] = True
                for chain in chains.values():
                    if chain[0] == NEVER:
                        chain[0] = clock["now"]
            yield when
            x_step(n, levels)
            yield post("core", 3 * unit * dp, 500)
            gathered(n)

        def begin_gather(n):
            z_send(n)
            launch((0, n), gather_chain(n))

        begin_gather(0)

        def halo_pairs(index, batch):
            if index % 2 == 0:
                up = (hsend.at[0], hrecv.at[0])
                down = (hsend.at[1], hrecv.at[1])
            else:
                ref = xpad if index == 1 else gpad
                part = pl.ds(batch * wb, wb)
                mine = ref.at[part, pl.ds(margin, seq)]
                up = (mine, ref.at[part, pl.ds(0, margin)])
                down = (mine, ref.at[part, pl.ds(margin + seq, margin)])
            return up, down

        def halo_send(index, batch=0):
            up, down = halo_pairs(index, batch)
            begin(rcopy(up[0], up[1], halo_s.at[index, batch, 0], halo_r.at[index, batch, 0],
                        dev(s, lax.rem(m + 1, mp), d)), m < mp - 1, "halo")
            begin(rcopy(down[0], down[1], halo_s.at[index, batch, 1], halo_r.at[index, batch, 1],
                        dev(s, lax.rem(m + mp - 1, mp), d)), m > 0, "halo")
            return post("z", (wb * seq * width * 2 / 1e3) if index % 2 else 98.0, 50)

        def halo_wait(index, batch=0, when=0.0):
            while chains and min(c[0] for c in chains.values()) <= when:
                first, key = min((c[0], key) for key, c in chains.items())
                clock["now"] = max(clock["now"], first)
                resume(key)
            clock["now"] = max(clock["now"], when)
            up, down = halo_pairs(index, batch)
            pl.when(m > 0)(lambda: received(up[1], halo_r.at[index, batch, 0]))
            pl.when(m < mp - 1)(lambda: received(down[1], halo_r.at[index, batch, 1]))

        def zero_edges(ref):
            @pl.when(m == 0)
            def _():
                ref[:, :margin] = jnp.zeros((nw, margin, width), BF)

            @pl.when(m == mp - 1)
            def _():
                ref[:, margin + seq:] = jnp.zeros((nw, margin, width), BF)

        def tile(j):
            return pl.ds(j * q_count, q_count)

        def stage_edges(ext):
            @pl.loop(0, nw)
            def _(w):
                for j in range(HALF):
                    last = ext[w, tile(PHASES + j), :].astype(F32)
                    hsend[0, w, pl.ds(j, 1), :] = last[q_count - 1:, :]
                    first = ext[w, tile(HALF + j), :].astype(F32)
                    hsend[1, w, pl.ds(j, 1), :] = first[:1, :]

        def fill_edges(ext):
            @pl.when(m == 0)
            def _():
                hrecv[0] = jnp.zeros((nw, 8, width), F32)

            @pl.when(m == mp - 1)
            def _():
                hrecv[1] = jnp.zeros((nw, 8, width), F32)

            @pl.loop(0, nw)
            def _(w):
                for j in range(HALF):
                    edge[j, pl.ds(8, q_count), :] = ext[w, tile(PHASES + j), :].astype(F32)
                    edge[j, pl.ds(7, 1), :] = hrecv[0, w, pl.ds(j, 1), :]
                    ext[w, tile(j), :] = edge[j, pl.ds(7, q_count), :].astype(BF)
                    edge[HALF + j, pl.ds(8, q_count), :] = ext[w, tile(HALF + j), :].astype(F32)
                    edge[HALF + j, pl.ds(8 + q_count, 1), :] = hrecv[1, w, pl.ds(j, 1), :]
                    ext[w, tile(HALF + PHASES + j), :] = edge[HALF + j, pl.ds(9, q_count), :].astype(BF)

        def to_phases(value, store):
            for c in range(width // 128):
                slab[c] = value[:, c * 128:(c + 1) * 128]
            for r in range(PHASES):
                store(r, jnp.concatenate(
                    [slab[c, pl.ds(r, q_count, stride=PHASES), :] for c in range(width // 128)], axis=1))

        def from_phases(value):
            for r in range(PHASES):
                for c in range(width // 128):
                    slab[c, pl.ds(r, q_count, stride=PHASES), :] = (
                        value[r * q_count:(r + 1) * q_count, c * 128:(c + 1) * 128])
            return jnp.concatenate([slab[c] for c in range(width // 128)], axis=1)

        def window_mask(w):
            return valid[s * nw + w].astype(F32)

        def shifted(ref, b, k, batch):
            first = k * (q_count if b == 0 else DILATION)
            if not isinstance(k, int):
                first = pl.multiple_of(first, TILE)
            if batch is None:
                return ref[:, pl.ds(first, seq), :].reshape(rows_all, width)
            return ref[pl.ds(batch * wb, wb), pl.ds(first, seq), :].reshape(wb * seq, width)

        def tap(b, k, batch=None):
            return shifted(xext if b == 0 else xpad, b, k, batch)

        def gtap(b, k, batch=None):
            return shifted(gpad, b, k, batch)

        def part_rows(batch):
            return slice(None) if batch is None else pl.ds(batch * wb * seq, wb * seq)

        def part_windows(batch):
            return (0, nw) if batch is None else (batch * wb, (batch + 1) * wb)

        def cols_of(n):
            return pl.ds(pl.multiple_of(n * COLS, COLS), COLS)

        def first_norm(b, batch=None):
            @pl.loop(*part_windows(batch))
            def _(w):
                if b == 0:
                    def keep(r, tile):
                        x0[w, pl.ds(r * q_count, q_count), :] = tile.astype(BF)
                    to_phases(x1[w].astype(F32), keep)
                    x = x0[w]
                else:
                    x = x1[w]
                hat, _r = norm_parts(x.astype(F32))
                n = (hat * gains[b, 0]).astype(BF)
                if b == 0:
                    xext[w, pl.ds(HALF * q_count, seq), :] = n
                else:
                    xpad[w, pl.ds(margin, seq), :] = n

        def conv_part(b, taps, batch, n):
            rows, cols = part_rows(batch), pl.ds(n * COLS, COLS)
            total = None
            for k in taps:
                wk = big[b, k, :, :, cols].reshape(width, COLS)
                term = dot(tap(b, k, batch), wk)
                total = term if total is None else total + term
            if taps[0]:
                total = total + acc[rows, cols]
            acc[rows, cols] = total

        def rows_of(w):
            return pl.ds(pl.multiple_of(w * seq, seq), seq)

        def middle(b, batch=None):
            x = x0 if b == 0 else x1

            @pl.loop(*part_windows(batch))
            def _(w):
                act, slope = gelu_and_slope(acc[rows_of(w), :])
                slope1[b, w] = slope.astype(BF)
                value = x[w].astype(F32) + window_mask(w) * act.astype(BF).astype(F32)
                if b == 0:
                    mid[w] = value
                midb[b, w] = value.astype(BF)
                hat, _r = norm_parts(value)
                ffn[b, rows_of(w), :] = (hat * gains[b, 1]).astype(BF)

        def up(b, batch, quarter, quarters):
            count = mp * width // COLS // quarters
            rows = part_rows(batch)

            @pl.loop(quarter * count, (quarter + 1) * count)
            def _(n):
                per = width // COLS
                wk = big[b, KERNEL + n // per, :, :, cols_of(lax.rem(n, per))].reshape(width, COLS)
                h, slope = gelu_and_slope(dot(ffn[b, rows, :], wk))
                hid[rows, cols_of(n)] = h.astype(BF)
                slo[rows, cols_of(n)] = slope.astype(BF)

        def down(b, batch):
            rows = part_rows(batch)

            @pl.loop(0, width // COLS)
            def _(n):
                total = None
                for mm in range(mp):
                    wk = big[b, KERNEL + mp + mm, :, :, cols_of(n)].reshape(width, COLS)
                    term = dot(hid[rows, mm * width:(mm + 1) * width], wk)
                    total = term if total is None else total + term
                acc[rows, cols_of(n)] = total

        def down_out(b, batch):
            @pl.loop(*part_windows(batch))
            def _(w):
                branch = window_mask(w) * acc[rows_of(w), :]
                if b == 0:
                    x1[w] = from_phases(mid[w] + branch).astype(BF)
                else:
                    x2[w] = (midb[b, w].astype(F32) + branch).astype(BF)

        def send_home(ref, target, b, index):
            dst = target.at[pl.ds(s * nw, nw)]

            @pl.when(s == b)
            def _():
                pltpu.make_async_copy(ref, dst, out_s.at[index]).start()

            @pl.when(s != b)
            def _():
                rcopy(ref, dst, out_s.at[index], out_r.at[index], sibling).start()

        def sent_home(ref, target, b, index):
            dst = target.at[pl.ds(s * nw, nw)]

            @pl.when(s == b)
            def _():
                pltpu.make_async_copy(ref, dst, out_s.at[index]).wait()
                received(target.at[pl.ds((1 - s) * nw, nw)], out_r.at[index])

            @pl.when(s != b)
            def _():
                rcopy(ref, dst, out_s.at[index], out_r.at[index], sibling).wait_send()

        def slot(b):
            return 2 if b == 1 else 1

        def branch_grad(b):
            @pl.loop(0, nw)
            def _(w):
                value = window_mask(w) * gout[w].astype(F32)
                low = value.astype(BF)
                gb[rows_of(w), :] = low
                tra[:, rows_of(w)] = low.T

        def transposed_ffn(b):
            @pl.loop(0, nw)
            def _(w):
                trb[:, rows_of(w)] = ffn[b, rows_of(w), :].T

        def wide(n):
            return pl.ds(pl.multiple_of(n * width, width), width)

        def down_grad(b):
            @pl.loop(0, mp)
            def _(n):
                part = dot(tra[...], hid[:, wide(n)])
                big[slot(b), KERNEL + mp + n] = part.astype(BF).reshape(mp, group_rows, width)

        def pre_grad(b):
            @pl.loop(0, mp * width // COLS)
            def _(n):
                per = width // COLS
                span = COLS // group_rows
                wk = big[b, KERNEL + mp + n // per, pl.ds(lax.rem(n, per) * span, span)].reshape(COLS, width)
                g = dot_nt(gb[...], wk) * slo[:, cols_of(n)].astype(F32)
                slo[:, cols_of(n)] = g.astype(BF)

        def up_grad(b):
            @pl.loop(0, mp)
            def _(n):
                part = dot(trb[...], slo[:, wide(n)])
                big[slot(b), KERNEL + n] = part.astype(BF).reshape(mp, group_rows, width)

        def ffn_grad(b):
            span = COLS // group_rows

            @pl.loop(0, width // COLS)
            def _(n):
                total = None
                for mm in range(mp):
                    wk = big[b, KERNEL + mm, pl.ds(n * span, span)].reshape(COLS, width)
                    term = dot_nt(slo[:, mm * width:(mm + 1) * width], wk)
                    total = term if total is None else total + term
                acc[:, cols_of(n)] = total

        def ffn_back(b, batch):
            @pl.loop(*part_windows(batch))
            def _(w):
                gf = acc[rows_of(w), :]
                hat, r = norm_parts(midb[b, w].astype(F32))
                gbuf[0, b, 1:2, :] += jnp.sum(gf * hat, axis=0, keepdims=True)
                gm = gout[w].astype(F32) + norm_back(gf * gains[b, 1], hat, r)
                mid[w] = gm
                ga = (window_mask(w) * gm).astype(BF).astype(F32)
                gc = ga * slope1[b, w].astype(F32)
                low = gc.astype(BF)
                if b == 0:
                    gpad[w, pl.ds(HALF * q_count, seq), :] = low
                else:
                    gpad[w, pl.ds(margin, seq), :] = low
                tra[:, rows_of(w)] = low.T

        def conv_grad(b, group):
            @pl.loop(group[0], group[0] + group[1])
            def _(k):
                part = dot(tra[...], tap(b, k))
                big[slot(b), k] = part.astype(BF).reshape(mp, group_rows, width)

        def in_grad(b, batch=None):
            span = COLS // group_rows
            rows = part_rows(batch)

            @pl.loop(0, width // COLS)
            def _(n):
                total = None
                for k in range(KERNEL):
                    wk = big[b, k, pl.ds(n * span, span)].reshape(COLS, width)
                    term = dot_nt(gtap(b, KERNEL - 1 - k, batch), wk)
                    total = term if total is None else total + term
                acc[rows, cols_of(n)] = total

        def in_back(b, batch):
            x = x0 if b == 0 else x1

            @pl.loop(*part_windows(batch))
            def _(w):
                gn = acc[rows_of(w), :]
                hat, r = norm_parts(x[w].astype(F32))
                gbuf[0, b, 0:1, :] += jnp.sum(gn * hat, axis=0, keepdims=True)
                value = mid[w] + norm_back(gn * gains[b, 0], hat, r)
                if b == 0:
                    x0[w] = from_phases(value).astype(BF)
                else:
                    ig1[w] = value.astype(BF)

                    def keep(r_, tile):
                        gout[w, pl.ds(r_ * q_count, q_count), :] = tile.astype(BF)
                    to_phases(value, keep)

        order = list(range(levels - 1, -1, -1))

        def region(ref, lead, kept, at):
            r0, rn, c0, cn = 0, half_rows, 0, width
            for j in range(levels - 1, kept - 1, -1):
                side = (at // (1 << j)) % 2
                if j >= 2:
                    cn //= 2
                    c0 = c0 + side * cn
                else:
                    rn //= 2
                    r0 = r0 + side * rn
            return r0, rn, c0, cn

        def grad_view(ref, group, half, part):
            j0, nj = group
            r0, rn, c0, cn = part
            rows = pl.ds(pl.multiple_of(half * half_rows + r0, TILE), rn)
            cols = slice(None) if cn == width else pl.ds(pl.multiple_of(c0, 128), cn)
            return ref.at[pl.ds(j0, nj), :, rows, cols]

        def add_into(group, half, part, other):
            j0, nj = group
            r0, rn, c0, cn = part
            rows = pl.ds(pl.multiple_of(half * half_rows + r0, TILE), rn)
            cols = slice(None) if cn == width else pl.ds(pl.multiple_of(c0, 128), cn)
            return j0, nj, rows, cols

        def accumulate(b, group, part, src):
            j0, nj, rows, cols = add_into(group, s, part, src)

            @pl.loop(j0, j0 + nj)
            def _(j):
                at = (slot(b), j, slice(None), rows, cols)
                big[at] = big[at] + src[j]

        def need_credit(n, which):
            if ggroups[n][0] == 0:
                pl.semaphore_wait(credit.at[n % per_grad, which], 1)

        def give_credit(n, which, device):
            if ggroups[n][0] == 1:
                pl.semaphore_signal(credit.at[n % per_grad, which], inc=1, device_id=device, device_id_type=MESH)

        def c_send(n):
            b, group = ggroups[n]
            need_credit(n, 0)
            src = grad_view(big.at[slot(b)], group, 1 - s, (0, half_rows, 0, width))
            begin(rcopy(src, recv_c.at[pl.ds(group[0], group[1])], rc_s.at[n], rc_r.at[n], sibling), None, n)

        def x_exchange(n, i):
            b, group = ggroups[n]
            j0, nj = group
            if i == 0:
                received(recv_c.at[pl.ds(j0, nj)], rc_r.at[n])
                accumulate(b, group, (0, half_rows, 0, width), recv_c)
                give_credit(n, 0, sibling)
            else:
                done = order[i - 1]
                received(recv_x[i - 1].at[pl.ds(j0, nj)], rx_r.at[n, i - 1])
                accumulate(b, group, region(None, None, done, place), recv_x[i - 1])
                give_credit(n, i, partner(done))
            if i < levels:
                j = order[i]
                need_credit(n, 1 + i)
                flip = place + (1 << j) - 2 * (1 << j) * bit(j)
                src = grad_view(big.at[slot(b)], group, s, region(None, None, j, flip))
                begin(rcopy(src, recv_x[i].at[pl.ds(j0, nj)], rx_s.at[n, i], rx_r.at[n, i], partner(j)), None, n)
            else:
                final = region(None, None, 0, place)
                for k in range(1, mp):
                    if n - per_grad not in z_first:
                        need_credit(n, levels + k)
                    rcopy(z_part(b, group, final, peer(k)), recv_z.at[k - 1, pl.ds(j0, nj)],
                          rz_s.at[n], rz_r.at[n], dev(s, peer(k), d)).start()
                held = recv_z.at[:, pl.ds(j0, nj)]
                sends.append((rcopy(held, held, rz_s.at[n], rz_r.at[n], sibling), None, n))

        def z_part(b, group, part, mm):
            j0, nj = group
            r0, rn, c0, cn = part
            rows = pl.ds(pl.multiple_of(s * half_rows + r0, TILE), rn)
            cols = slice(None) if cn == width else pl.ds(pl.multiple_of(c0, 128), cn)
            if j0 < KERNEL:
                return big.at[slot(b), pl.ds(j0, nj), mm, rows, cols]
            return big.at[slot(b), j0 + mm, :, rows, cols]

        def finish(n):
            b, group = ggroups[n]
            j0, nj = group
            final = region(None, None, 0, place)
            r0, rn, c0, cn = final
            received(recv_z.at[:, pl.ds(j0, nj)], rz_r.at[n])
            total = z_part(b, group, final, m)[...].astype(F32)
            for k in range(1, mp):
                total = total + recv_z[k - 1, pl.ds(j0, nj)].astype(F32)
            if n + per_grad not in z_first:
                for k in range(1, mp):
                    give_credit(n, levels + k, dev(s, peer(mp - k), d))
            piece[b, pl.ds(j0, nj)] = total.astype(BF)
            spread(n)

        def spread(n):
            b, group = ggroups[n]
            j0, nj = group
            r0, rn, c0, cn = region(None, None, 0, place)
            rows = pl.ds(pl.multiple_of(s * half_rows + r0, TILE), rn)
            cols = slice(None) if cn == width else pl.ds(pl.multiple_of(c0, 128), cn)
            dst = fin.at[pl.ds(j0, nj), rows, cols]
            src = piece.at[b, pl.ds(j0, nj)]

            pl.when(s == b)(pltpu.make_async_copy(src, dst, rf_r.at[0]).start)
            begin(rcopy(src, dst, rf_s.at[n, 0], rf_r.at[0], sibling), s != b, n)
            for o in range(1, dp):
                begin(rcopy(src, dst, rf_s.at[n, o], rf_r.at[0], dev(b, m, across(o))), None, n)

        def shard_part(n, mm, part):
            b, (j0, nj) = ggroups[n]
            r0, rn, c0, cn = part
            rows = pl.ds(pl.multiple_of(s * half_rows + r0, TILE), rn)
            cols = slice(None) if cn == width else pl.ds(pl.multiple_of(c0, 128), cn)
            if j0 < KERNEL:
                return (slot(b), pl.ds(j0, nj), mm, rows, cols)
            return (slot(b), j0 + mm, slice(None), rows, cols)

        side = (0, half_rows, 0, width)

        def z_pair(stage):
            if stage == 0:
                other = m + 1 - 2 * lax.rem(m, 2)
                return other, [(lax.rem(other, 2) + 2 * i, lax.rem(m, 2) + 2 * i, i) for i in range(2)]
            other = m + 2 - 4 * (m // 2)
            return other, [(other, m, 2)]

        def z_landing(n, i):
            return recv_zf.at[z_first[n], i, pl.ds(0, ggroups[n][1][1])]

        def z_first_send(n, stage):
            other, parts = z_pair(stage)
            at = z_order.index(n)
            for theirs, _, i in parts:
                begin(rcopy(big.at[shard_part(n, theirs, side)], z_landing(n, i),
                            zf_s.at[at, i], zf_r.at[at, i], dev(s, other, d)), None, n)

        def z_first_take(n, stage):
            other, parts = z_pair(stage)
            at = z_order.index(n)
            for _, mine, i in parts:
                received(z_landing(n, i), zf_r.at[at, i])
                where = shard_part(n, mine, side)
                big[where] = big[where] + recv_zf[z_first[n], i, pl.ds(0, ggroups[n][1][1])]

        def z_first_cross(n, i):
            j0, nj = ggroups[n][1]
            if i:
                done = order[i - 1]
                received(recv_x[i - 1].at[j0, pl.ds(0, nj)], rx_r.at[n, i - 1])
                where = shard_part(n, m, region(None, None, done, place))
                big[where] = big[where] + recv_x[i - 1][j0, pl.ds(0, nj)]
                give_credit(n, i, partner(done))
            if i < levels:
                j = order[i]
                need_credit(n, 1 + i)
                flip = place + (1 << j) - 2 * (1 << j) * bit(j)
                begin(rcopy(big.at[shard_part(n, m, region(None, None, j, flip))], recv_x[i].at[j0, pl.ds(0, nj)],
                            rx_s.at[n, i], rx_r.at[n, i], partner(j)), None, n)

        def z_first_chain(n):
            b, group = ggroups[n]
            j0, nj = group
            size = nj * width * width * 2 / 1e3
            c_send(n)
            yield post("core", size / 2, 500)
            received(recv_c.at[pl.ds(j0, nj)], rc_r.at[n])
            accumulate(b, group, side, recv_c)
            give_credit(n, 0, sibling)
            for stage in range(2):
                z_first_send(n, stage)
                yield post("z", size / 4 / (1 + stage), 50)
                z_first_take(n, stage)
            for i in range(levels):
                z_first_cross(n, i)
                yield post("xy", size / 16 / (1 << i), 100)
            z_first_cross(n, levels)
            piece[b, pl.ds(j0, nj)] = big[shard_part(n, m, region(None, None, 0, place))]
            spread(n)
            post("xy", size / 2 / dp / mp * dp / 2, 100)

        def across(o):
            out = d
            for j in range(levels):
                if (o >> j) & 1:
                    out = out + (1 << j) - 2 * (1 << j) * ((d // (1 << j)) % 2)
            return out

        def reduce_chain(n):
            if n in z_first:
                yield from z_first_chain(n)
                return
            b, group = ggroups[n]
            size = group[1] * width * width * 2 / 1e3
            c_send(n)
            yield post("core", size / 2, 500)
            for i in range(levels):
                x_exchange(n, i)
                yield post("xy", size / 4 / (1 << i), 100)
            x_exchange(n, levels)
            yield post("z", 2 * size / 2 / dp, 100)
            finish(n)
            post("xy", size / 2 / dp / mp * dp / 2, 100)

        first, second = range(per_block), range(per_block, 2 * per_block)
        for copy in loads:
            copy.wait()
        gbuf[0] = jnp.zeros((2, 8, width), F32)
        received(gains.at[1 - s, 0], gn_r.at[0])
        received(gains.at[1 - s, 1], gn_r.at[levels + mp])
        work(2.5, first_norm, 0)
        stage_edges(xext)
        arrived = halo_send(0)
        for n in range(1, per_block):
            begin_gather(n)
        halo_wait(0, 0, arrived)
        work(0.5, fill_edges, xext)
        for g in range(3):
            complete([(0, g)])
            for n in range(width // COLS):
                work(1.0, conv_part, 0, range(3 * g, 3 * g + 3), None, n)
        for batch in range(batches):
            work(1.0, middle, 0, batch)
        complete([(0, 3)])
        for quarter in range(4):
            work(1.0, up, 0, None, quarter, 4)
        spill = [pltpu.make_async_copy(hid, sp_hid, loc.at[4]), pltpu.make_async_copy(slo, sp_slo, loc.at[5])]
        for copy in spill:
            copy.start()
        complete([(0, 4)])
        arrived = []
        for batch in range(batches):
            work(0.7, down, 0, batch)
            work(1.3, down_out, 0, batch)
            work(0.7, first_norm, 1, batch)
            arrived.append(halo_send(1, batch))
        send_home(x1, blk, 0, 0)
        zero_edges(xpad)
        zero_edges(gpad)
        work(2.5, branch_grad, 1)
        for batch in range(batches):
            halo_wait(1, batch, arrived[batch])
            if batch == 0:
                complete([(0, per_block + g) for g in range(3)])
            for n in range(width // COLS):
                work(1.0, conv_part, 1, range(KERNEL), batch, n)
            work(1.0, middle, 1, batch)
            if batch == 0:
                for copy in spill:
                    copy.wait()
                complete([(0, per_block + 3)])
            for half in range(2):
                work(0.7, up, 1, batch, half, 2)
        work(2.2, down_grad, 1)
        launch((1, 0), reduce_chain(0))
        work(1.5, transposed_ffn, 1)
        complete([(0, per_block + 4)])
        work(3.0, pre_grad, 1)
        work(2.2, up_grad, 1)
        launch((1, 1), reduce_chain(1))
        work(2.5, ffn_grad, 1)
        arrived = []
        for batch in range(batches):
            work(1.2, ffn_back, 1, batch)
            arrived.append(halo_send(3, batch))
        for g, group in enumerate(back_groups):
            work(0.7 * group[1], conv_grad, 1, group)
            launch((1, 2 + g), reduce_chain(2 + g))
        work(2.0, down, 1, None)
        work(1.0, down_out, 1, None)
        send_home(x2, blk, 1, 1)
        fetch = [pltpu.make_async_copy(sp_hid, hid, loc.at[6]), pltpu.make_async_copy(sp_slo, slo, loc.at[7])]
        for copy in fetch:
            copy.start()
        for batch in range(batches):
            halo_wait(3, batch, arrived[batch])
            work(1.8, in_grad, 1, batch)
            work(1.0, in_back, 1, batch)
        send_home(ig1, ing, 1, 3)
        flush(("gather", 1))
        work(2.5, branch_grad, 0)
        for copy in fetch:
            copy.wait()
        work(2.2, down_grad, 0)
        launch((1, per_grad), reduce_chain(per_grad))
        work(1.5, transposed_ffn, 0)
        work(3.0, pre_grad, 0)
        work(2.2, up_grad, 0)
        launch((1, per_grad + 1), reduce_chain(per_grad + 1))
        flush("halo")
        work(2.5, ffn_grad, 0)
        for batch in range(batches):
            work(1.2, ffn_back, 0, batch)
        stage_edges(gpad)
        arrived = halo_send(2)
        for g, group in enumerate(back_groups):
            work(0.7 * group[1], conv_grad, 0, group)
            launch((1, per_grad + 2 + g), reduce_chain(per_grad + 2 + g))
        halo_wait(2, 0, arrived)
        work(0.5, fill_edges, gpad)
        work(5.0, in_grad, 0)
        for batch in range(batches):
            work(1.0, in_back, 0, batch)
        send_home(x0, ing, 0, 2)

        def gain_chain():
            begin(rcopy(gbuf.at[0], grecv.at[0], gn_s.at[1], gn_r.at[1], sibling))
            for i in range(levels + 1):
                yield clock["now"] + LATENCY
                received(grecv.at[i], gn_r.at[1 + i])
                gbuf[i + 1] = gbuf[i] + grecv[i]
                if i < levels:
                    begin(rcopy(gbuf.at[i + 1], grecv.at[i + 1], gn_s.at[2 + i], gn_r.at[2 + i], partner(i)))
            for k in range(1, mp):
                at = levels + k
                begin(rcopy(gbuf.at[levels + 1], grecv.at[at], gn_s.at[1 + at], gn_r.at[1 + at], dev(s, peer(k), d)))
            yield clock["now"] + 2 * LATENCY
            total = gbuf[levels + 1]
            for k in range(1, mp):
                at = levels + k
                received(grecv.at[at], gn_r.at[1 + at])
                total = total + grecv[at]
            gbuf[levels + 2] = total

        launch((2, 0), gain_chain())
        for n in range(nwg):
            z_flush(n)
        flush(("gather", 0))
        flush("halo")
        for n in range(ngg):
            if (1, n) not in chains:
                flush(n)
        complete(list(chains))
        out = pltpu.make_async_copy(
            gbuf.at[levels + 2, s, :, pl.ds(pl.multiple_of(m * group_rows, group_rows), group_rows)], gout_sum, loc.at[0])
        out.start()
        received(fin, rf_r.at[0])
        flush()
        sent_home(x1, blk, 0, 0)
        sent_home(x2, blk, 1, 1)
        sent_home(x0, ing, 0, 2)
        sent_home(ig1, ing, 1, 3)
        out.wait()

    vm = pltpu.VMEM
    dma = pltpu.SemaphoreType.DMA
    plain = (nw, seq, width)
    flat = (rows_all, width)

    def recv_shape(i):
        r, c = half_rows, width
        for j in range(levels - 1, levels - 2 - i, -1):
            if j >= 2:
                c //= 2
            else:
                r //= 2
        return (nblk, mp, r, c)

    piece_shape = (nblk, recv_shape(levels - 1)[2], recv_shape(levels - 1)[3])
    scratch = [
        vm((3, nblk, mp, group_rows, width), BF),
        vm((nblk, mp, half_rows, width), BF),
        vm((mp - 1,) + piece_shape, BF),
        vm((max(1, min(2, len(Z_FIRST))), 3, mp, half_rows, width), BF),
        vm((2,) + piece_shape, BF),
        vm((nw, 2 * seq, width), BF),
        vm((nw, 2 * margin + seq, width), BF),
        vm((nw, 2 * margin + seq, width), BF),
        vm((rows_all, mp * width), BF),
        vm((rows_all, mp * width), BF),
        vm(plain, BF),
        vm(plain, BF),
        vm(plain, BF),
        vm((2,) + plain, BF),
        vm((2,) + flat, BF),
        vm((2,) + plain, BF),
        vm(plain, BF),
        vm(flat, BF),
        vm((width, rows_all), BF),
        vm((width, rows_all), BF),
        vm(flat, F32),
        vm(plain, F32),
        vm(plain, BF),
        vm((2, 2, 1, width), F32),
        vm((width // 128, seq, 128), F32),
        vm((2 * HALF, q_count + 16, width), F32),
        vm((2, nw, 8, width), F32),
        vm((2, nw, 8, width), F32),
        vm((levels + 3, 2, 8, width), F32),
        vm((levels + mp, 2, 8, width), F32),
    ] + [vm(recv_shape(i), BF) for i in range(levels)] + [
        dma((per_block, mp - 1, 2)), dma((nwg, mp - 1)), dma((nwg,)),
        dma((nwg, levels)), dma((nwg, levels)),
        dma((nwg,)), dma((nwg,)),
        dma((per_block,)), dma((per_block,)), dma((per_block,)),
        dma((ngg,)), dma((ngg,)),
        dma((ngg, levels)), dma((ngg, levels)),
        dma((ngg,)), dma((ngg,)),
        dma((1 + len(z_first), 3)), dma((1 + len(z_first), 3)),
        dma((ngg, dp)), dma((1,)),
        dma((1 + levels + mp + 1,)), dma((1 + levels + mp + 1,)),
        dma((4, batches, 2)), dma((4, batches, 2)),
        dma((4,)), dma((4,)),
        dma((8,)),
        pltpu.SemaphoreType.REGULAR((per_grad, levels + mp)),
    ]
    return body, scratch


def per_device(tokens, valid, conv_weight, gain_one, gain_two, up_weight, down_weight, cotangent):
    mp = lax.axis_size("mp")
    dp = lax.axis_size("dp")
    windows, seq, width = tokens.shape
    nw = windows // 2
    rows = width // mp
    body, scratch = make_kernel(mp, dp, nw, seq, width)
    conv = conv_weight[0].reshape(KERNEL, mp, rows, rows)
    up = up_weight[0].reshape(mp, rows, width)
    down = down_weight[0].reshape(mp, rows, width)
    nblk = KERNEL + 2 * mp
    anywhere = pl.BlockSpec(memory_space=pl.ANY)
    blk, ing, fin, sums, _, _ = pl.pallas_call(
        body,
        out_shape=(
            jax.ShapeDtypeStruct(tokens.shape, BF),
            jax.ShapeDtypeStruct(tokens.shape, BF),
            jax.ShapeDtypeStruct((nblk, rows, width), BF),
            jax.ShapeDtypeStruct((8, rows), F32),
            jax.ShapeDtypeStruct((nw * seq, mp * width), BF),
            jax.ShapeDtypeStruct((nw * seq, mp * width), BF),
        ),
        in_specs=[anywhere] * 2 + [pl.BlockSpec(memory_space=pltpu.SMEM)] + [anywhere] * 5,
        out_specs=[anywhere] * 6,
        scratch_shapes=scratch,
        compiler_params=pltpu.CompilerParams(
            collective_id=0, has_side_effects=True, vmem_limit_bytes=64 * 1024 * 1024 - 64 * 1024
        ),
    )(tokens, cotangent, valid, gain_one, gain_two, conv, up, down)
    return finalize(mp, blk, ing, fin, sums)


def finalize(mp, blk, ing, fin, sums):
    nblk, rows, width = fin.shape

    def body(blk_in, ing_in, fin_in, sums_in, blk_out, ing_out, conv_out, one_out, two_out, up_out, down_out,
             held, conv, up, down, acts, sem):
        moves = [pltpu.make_async_copy(blk_in, acts.at[0], sem.at[0]),
                 pltpu.make_async_copy(ing_in, acts.at[1], sem.at[1])]
        parts = [(0, KERNEL), (KERNEL, mp), (KERNEL + mp, mp)]
        reads = [pltpu.make_async_copy(fin_in.at[pl.ds(a, n)], held.at[pl.ds(a, n)], sem.at[2 + i])
                 for i, (a, n) in enumerate(parts)]
        for copy in moves + reads:
            copy.start()
        one_out[...] = sums_in[0:1, :]
        two_out[...] = sums_in[1:2, :]
        writes = []

        def store(src, dst, at):
            copy = pltpu.make_async_copy(src, dst, sem.at[at])
            copy.start()
            writes.append(copy)

        for i, out in enumerate((blk_out, ing_out)):
            moves[i].wait()
            store(acts.at[i], out.at[0], 10 + i)
        reads[0].wait()
        for k in range(KERNEL):
            conv[k] = held[k].astype(F32).T
            if k % 3 == 2:
                store(conv.at[pl.ds(k - 2, 3)], conv_out.at[0, pl.ds(k - 2, 3)], 5 + k // 3)
        reads[2].wait()
        for j in range(mp):
            down[:, j * rows:(j + 1) * rows] = held[KERNEL + mp + j].astype(F32).T
        store(down, down_out.at[0], 8)
        reads[1].wait()
        for j in range(mp):
            up[j * rows:(j + 1) * rows, :] = held[KERNEL + j].astype(F32)
        store(up, up_out.at[0], 9)
        for copy in writes:
            copy.wait()

    anywhere = pl.BlockSpec(memory_space=pl.ANY)
    vmem = pl.BlockSpec(memory_space=pltpu.VMEM)
    square = (mp * rows, width)
    return pl.pallas_call(
        body,
        out_shape=(
            jax.ShapeDtypeStruct((1,) + blk.shape, BF),
            jax.ShapeDtypeStruct((1,) + ing.shape, BF),
            jax.ShapeDtypeStruct((1, KERNEL, width, rows), F32),
            jax.ShapeDtypeStruct((1, rows), F32),
            jax.ShapeDtypeStruct((1, rows), F32),
            jax.ShapeDtypeStruct((1,) + square, F32),
            jax.ShapeDtypeStruct((1, width, mp * rows), F32),
        ),
        in_specs=[anywhere, anywhere, anywhere, vmem],
        out_specs=[anywhere, anywhere, anywhere, vmem, vmem, anywhere, anywhere],
        scratch_shapes=[
            pltpu.VMEM(fin.shape, BF),
            pltpu.VMEM((KERNEL, width, rows), F32),
            pltpu.VMEM(square, F32),
            pltpu.VMEM((width, mp * rows), F32),
            pltpu.VMEM((2,) + blk.shape, BF),
            pltpu.SemaphoreType.DMA((12,)),
        ],
        compiler_params=pltpu.CompilerParams(vmem_limit_bytes=64 * 1024 * 1024 - 64 * 1024),
    )(blk, ing, fin, sums)


def solution(mesh):
    in_specs = (
        P("dp", "mp", None),
        P("dp"),
        P("section", None, None, "mp"),
        P("section", None),
        P("section", None),
        P("section", None, "mp"),
        P("section", "mp", None),
        P("dp", "mp", None),
    )
    out_specs = (
        P("section", "dp", "mp", None),
        P("section", "dp", "mp", None),
        P("section", None, None, "mp"),
        P("section", "mp"),
        P("section", "mp"),
        P("section", None, "mp"),
        P("section", "mp", None),
    )
    return jax.shard_map(
        per_device, mesh=mesh, in_specs=in_specs, out_specs=out_specs, check_vma=False
    )
```

time: 1970 us -> 213 us (0.11)
  waiting for transfers between devices: 1010 us -> 0 us
  matrix products: 367 us -> 0 us
  other arithmetic: 250 us -> 0 us
  Pallas kernels: 0 us -> 212 us
  local copies, waits for them, and re-layouts: 202 us -> 0 us
  starting transfers between devices: 81.2 us -> 0 us
  blocking collectives: 25.7 us -> 0 us
    all_gather x23 -> x0, waiting for transfers between devices: 404 us -> none  [the longest x7 169 us: backward_block(): branch_all = lax.all_gather(grad_branch, 'mp', axis=0, tiled=True)]
    dot_general x242 -> x0, matrix products: 367 us -> none  [the longest x63 113 us: backward_block(): jnp.einsum('swd,swe->de', window, grad_conv, preferred_element_type=jnp.f...]
    psum x1 -> x0, waiting for transfers between devices: 277 us -> none  [per_device(): lax.psum(as_sent(parts), 'dp')]
    pallas_call x0 -> x2, Pallas kernels: none -> 212 us  [the longest x1 206 us: per_device(): pl.pallas_call(body, out_shape=(jax.ShapeDtypeStruct(tokens.shape, BF), j...]
    reduce_scatter x22 -> x0, waiting for transfers between devices: 204 us -> none  [the longest x7 135 us: backward_block(): lax.psum_scatter(total.astype(jnp.bfloat16), 'mp', scatter_dimension=0, t...]
    all_to_all x15 -> x0, waiting for transfers between devices: 123 us -> none  [the longest x8 84.9 us: forward_block(): lax.all_to_all(activated, 'mp', split_axis=0, concat_axis=2, tiled=True)]
    convert_element_type x62 -> x0, other arithmetic: 86.8 us -> none  [the longest x21 31.1 us: backward_block(): grad_conv = conv_pull(act_all.astype(jnp.float32))[0].astype(jnp.bfloat16)]
    dynamic_update_slice x36 -> x0, other arithmetic: 78.9 us -> none  [the longest x21 46.4 us: per_device(): lax.dynamic_update_index_in_dim(buffer, value, tick % 3, 0)]
  transfers between devices with their start and end apart: 74 -> 0, of which waited for: 58 -> 0; matrix products, arithmetic and copies ran while one was open for 28% -> 0% of each run, Pallas kernels for 0% -> 0%
where the time goes in v1:
time: 213 us
  Pallas kernels  212 us (100%)
    pallas_call x1, Pallas kernels, per_device(): pl.pallas_call(body, out_shape=(jax.ShapeDtypeStruct(tokens.shape, BF), j...  206 us
    pallas_call x1, Pallas kernels, finalize(): pl.pallas_call(body, out_shape=(jax.ShapeDtypeStruct((1,) + blk.shape, BF...  5.79 us

profile of v1, /device:TPU:0, one launch (start us, length us, event | category | flops | bytes accessed | tf_op | source)
XLA Modules:
  0.0 212.8 jit_solution(7650065367160916216)
XLA Ops:
  0.6 206.2 %shard_map.135 = (bf16[12,128,512]{2,1,0:T(8,128)(2,1)}, bf16[12,128,512]{2,1,0:T(8,128)(2,1)}, bf16[17,128,512]{2,1,0:T(8,128)(2,1)}, f32[8,128]{1,0:T(8,128)},...) custom-call(bf16[12,128,512]{2,1,0:T(8,128)(2,1)} %tok.1, bf16[12,128,512]{2,1,0:T(8,128)(2,1)} %cot.1, s32[12]{0:T(128)} %valid.1, ...), custom_call_target="tpu_custom_call" | custom-call | tf_op jit(solution)/shard_map/pallas_call | solution.py:1102
  206.8 5.8 %shard_map.136 = (bf16[1,12,128,512]{3,2,1,0:T(8,128)(2,1)}, bf16[1,12,128,512]{3,2,1,0:T(8,128)(2,1)}, f32[1,9,512,128]{3,2,1,0:T(8,128)}, f32[1,128]{1,0:T(1,1...) custom-call(bf16[12,128,512]{2,1,0:T(8,128)(2,1)} %get-tuple-element.11.blk_in, ...), custom_call_target="tpu_custom_call" | custom-call | tf_op jit(solution)/shard_map/pallas_call | solution.py:1165

commit v2 on v1

--- a/solution.py
+++ b/solution.py
@@ -18,16 +18,16 @@
 MESH = pl.DeviceIdType.MESH
 LATENCY = 2.0
 NEVER = 1e9
+WIDE_Z = 0
 AHEAD = 1.0
 Z_FIRST = (7,)
 
 
 def gelu_and_slope(v):
     v2 = v * v
-    t = jnp.tanh(v * (C0 + (C0 * C1) * v2))
-    h = 0.5 + 0.5 * t
-    slope = h + v * (1.0 - t * t) * (0.5 * C0 + (1.5 * C0 * C1) * v2)
-    return v * h, slope
+    h = 0.5 + 0.5 * jnp.tanh(v * (C0 + (C0 * C1) * v2))
+    out = v * h
+    return out, h + out * (1.0 - h) * (2.0 * C0 + (6.0 * C0 * C1) * v2)
 
 
 def norm_parts(values):
@@ -69,7 +69,7 @@
     z_order = list(Z_FIRST)
     assert len(z_order) <= 2
     z_first = {g: i % 2 for i, g in enumerate(z_order)}
-    batches = 3 if nw % 3 == 0 else 1
+    batches = 2 if nw % 2 == 0 else 1
     wb = nw // batches
     nwg, ngg = len(wgroups), len(ggroups)
     per_block = len(conv_groups) + 2
@@ -79,7 +79,7 @@
              blk, ing, fin, gout_sum, sp_hid, sp_slo,
              big, recv_c, recv_z, recv_zf, piece, xext, xpad, gpad, hid, slo, x0, x1, x2, midb, ffn,
              slope1, gout, gb, tra, trb, acc, mid, ig1, gains, slab, edge, hsend, hrecv,
-             gbuf, grecv, *rest):
+             gbuf, grecv, gz, *rest):
         recv_x = rest[:levels]
         (agz_s, agz_r, agf_s, agx_s, agx_r, agk_s, agk_r, own_l, own_s, own_r, rc_s, rc_r, rx_s, rx_r,
          rz_s, rz_r, zf_s, zf_r, rf_s, rf_r, gn_s, gn_r, halo_s, halo_r, out_s, out_r, loc, credit) = rest[levels:]
@@ -192,7 +192,11 @@
             local.start()
             own.append(local)
         begin(rcopy(one_in, gains.at[s, 0], gn_s.at[0], gn_r.at[0], sibling))
-        begin(rcopy(two_in, gains.at[s, 1], gn_s.at[levels + mp], gn_r.at[levels + mp], sibling))
+        begin(rcopy(two_in, gains.at[s, 1], gn_s.at[1], gn_r.at[1], sibling))
+
+        def z_level(n):
+            b, group = wgroups[n]
+            return WIDE_Z if b == 1 and group[0] >= KERNEL and levels == 2 else 0
 
         def z_copies(n):
             b, group = wgroups[n]
@@ -201,8 +205,8 @@
             for k in (2, 1, 3):
                 for half in range(2):
                     copy = rcopy(
-                        sub(own_source(group), half, place_of(half), 0),
-                        sub(shard_view(b, group, m), half, place_of(half), 0),
+                        sub(own_source(group), half, place_of(half), z_level(n)),
+                        sub(shard_view(b, group, m), half, place_of(half), z_level(n)),
                         agz_s.at[i, k - 1, half], agz_r.at[n, k - 1], dev(half, peer(k), d))
                     out.append((copy, None if k == 2 else (m != 3 if k == 1 else m != 0)))
             return out
@@ -230,7 +234,7 @@
 
         def z_forward(n):
             b, group = wgroups[n]
-            held = sub(shard_view(b, group, peer(mp - 2)), s, place, 0)
+            held = sub(shard_view(b, group, peer(mp - 2)), s, place, z_level(n))
             received(held, agz_r.at[n, 1])
             for at, to, k in ((2, 3, 3), (1, 0, 1)):
                 begin(rcopy(held, held, agf_s.at[n], agz_r.at[n, k - 1], dev(s, to, d)), m == at, ("gather", b))
@@ -247,9 +251,9 @@
 
         def x_step(n, level):
             b, group = wgroups[n]
-            if level == 0:
+            if level == z_level(n):
                 for k in (1, 3):
-                    received(sub(shard_view(b, group, peer(mp - k)), s, place, 0), agz_r.at[n, k - 1])
+                    received(sub(shard_view(b, group, peer(mp - k)), s, place, level), agz_r.at[n, k - 1])
             else:
                 received(foreign(n, s, place, level - 1), agx_r.at[n, level - 1])
             if level < levels:
@@ -324,7 +328,7 @@
         def gather_chain(n):
             b, group = wgroups[n]
             unit = (group[1] * width * group_rows if group[0] < KERNEL else width * width) * 2 / (2 * dp) / 1e3
-            yield post("z", 6 * unit, 100)
+            yield post("z", 6 * unit * (1 << z_level(n)), 100)
             if n == per_block - 2:
                 for later in range(per_block, nwg):
                     begin_gather(later)
@@ -332,10 +336,9 @@
                 yield NEVER
             z_forward(n)
             yield clock["now"] + LATENCY
-            x_step(n, 0)
-            when = post("xy", 3 * unit, 100)
-            for level in range(1, levels):
-                yield when
+            for level in range(z_level(n), levels):
+                if level > z_level(n):
+                    yield when
                 x_step(n, level)
                 when = post("xy", 3 * unit * (1 << level), 100)
             if n == per_block - 1:
@@ -483,11 +486,8 @@
 
         def conv_part(b, taps, batch, n):
             rows, cols = part_rows(batch), pl.ds(n * COLS, COLS)
-            total = None
-            for k in taps:
-                wk = big[b, k, :, :, cols].reshape(width, COLS)
-                term = dot(tap(b, k, batch), wk)
-                total = term if total is None else total + term
+            wk = big[b, pl.ds(taps[0], len(taps)), :, :, cols].reshape(len(taps) * width, COLS)
+            total = dot(jnp.concatenate([tap(b, k, batch) for k in taps], axis=1), wk)
             if taps[0]:
                 total = total + acc[rows, cols]
             acc[rows, cols] = total
@@ -526,12 +526,8 @@
 
             @pl.loop(0, width // COLS)
             def _(n):
-                total = None
-                for mm in range(mp):
-                    wk = big[b, KERNEL + mp + mm, :, :, cols_of(n)].reshape(width, COLS)
-                    term = dot(hid[rows, mm * width:(mm + 1) * width], wk)
-                    total = term if total is None else total + term
-                acc[rows, cols_of(n)] = total
+                wk = big[b, pl.ds(KERNEL + mp, mp), :, :, cols_of(n)].reshape(mp * width, COLS)
+                acc[rows, cols_of(n)] = dot(hid[rows, :], wk)
 
         def down_out(b, batch):
             @pl.loop(*part_windows(batch))
@@ -610,19 +606,15 @@
 
             @pl.loop(0, width // COLS)
             def _(n):
-                total = None
-                for mm in range(mp):
-                    wk = big[b, KERNEL + mm, pl.ds(n * span, span)].reshape(COLS, width)
-                    term = dot_nt(slo[:, mm * width:(mm + 1) * width], wk)
-                    total = term if total is None else total + term
-                acc[:, cols_of(n)] = total
+                wk = [big[b, KERNEL + mm, pl.ds(n * span, span)].reshape(COLS, width) for mm in range(mp)]
+                acc[:, cols_of(n)] = dot_nt(slo[...], jnp.concatenate(wk, axis=1))
 
         def ffn_back(b, batch):
             @pl.loop(*part_windows(batch))
             def _(w):
                 gf = acc[rows_of(w), :]
                 hat, r = norm_parts(midb[b, w].astype(F32))
-                gbuf[0, b, 1:2, :] += jnp.sum(gf * hat, axis=0, keepdims=True)
+                gbuf[0, 2 * b + 1:2 * b + 2, :] += jnp.sum(gf * hat, axis=0, keepdims=True)
                 gm = gout[w].astype(F32) + norm_back(gf * gains[b, 1], hat, r)
                 mid[w] = gm
                 ga = (window_mask(w) * gm).astype(BF).astype(F32)
@@ -640,18 +632,15 @@
                 part = dot(tra[...], tap(b, k))
                 big[slot(b), k] = part.astype(BF).reshape(mp, group_rows, width)
 
-        def in_grad(b, batch=None):
+        def in_grad(b, batch=None, half=None):
             span = COLS // group_rows
             rows = part_rows(batch)
 
-            @pl.loop(0, width // COLS)
+            @pl.loop(*((0, width // COLS) if half is None else (half, half + 1)))
             def _(n):
-                total = None
-                for k in range(KERNEL):
-                    wk = big[b, k, pl.ds(n * span, span)].reshape(COLS, width)
-                    term = dot_nt(gtap(b, KERNEL - 1 - k, batch), wk)
-                    total = term if total is None else total + term
-                acc[rows, cols_of(n)] = total
+                wk = [big[b, k, pl.ds(n * span, span)].reshape(COLS, width) for k in range(KERNEL)]
+                g = [gtap(b, KERNEL - 1 - k, batch) for k in range(KERNEL)]
+                acc[rows, cols_of(n)] = dot_nt(jnp.concatenate(g, axis=1), jnp.concatenate(wk, axis=1))
 
         def in_back(b, batch):
             x = x0 if b == 0 else x1
@@ -660,7 +649,7 @@
             def _(w):
                 gn = acc[rows_of(w), :]
                 hat, r = norm_parts(x[w].astype(F32))
-                gbuf[0, b, 0:1, :] += jnp.sum(gn * hat, axis=0, keepdims=True)
+                gbuf[0, 2 * b:2 * b + 1, :] += jnp.sum(gn * hat, axis=0, keepdims=True)
                 value = mid[w] + norm_back(gn * gains[b, 0], hat, r)
                 if b == 0:
                     x0[w] = from_phases(value).astype(BF)
@@ -739,38 +728,31 @@
                 flip = place + (1 << j) - 2 * (1 << j) * bit(j)
                 src = grad_view(big.at[slot(b)], group, s, region(None, None, j, flip))
                 begin(rcopy(src, recv_x[i].at[pl.ds(j0, nj)], rx_s.at[n, i], rx_r.at[n, i], partner(j)), None, n)
-            else:
-                final = region(None, None, 0, place)
-                for k in range(1, mp):
-                    if n - per_grad not in z_first:
-                        need_credit(n, levels + k)
-                    rcopy(z_part(b, group, final, peer(k)), recv_z.at[k - 1, pl.ds(j0, nj)],
-                          rz_s.at[n], rz_r.at[n], dev(s, peer(k), d)).start()
-                held = recv_z.at[:, pl.ds(j0, nj)]
-                sends.append((rcopy(held, held, rz_s.at[n], rz_r.at[n], sibling), None, n))
-
-        def z_part(b, group, part, mm):
-            j0, nj = group
-            r0, rn, c0, cn = part
-            rows = pl.ds(pl.multiple_of(s * half_rows + r0, TILE), rn)
-            cols = slice(None) if cn == width else pl.ds(pl.multiple_of(c0, 128), cn)
-            if j0 < KERNEL:
-                return big.at[slot(b), pl.ds(j0, nj), mm, rows, cols]
-            return big.at[slot(b), j0 + mm, :, rows, cols]
-
-        def finish(n):
-            b, group = ggroups[n]
-            j0, nj = group
-            final = region(None, None, 0, place)
-            r0, rn, c0, cn = final
+
+        def z_send_pieces(n):
+            j0, nj = ggroups[n][1]
+            for k in range(1, mp):
+                if n - per_grad not in z_first:
+                    need_credit(n, levels + k)
+                rcopy(big.at[shard_part(n, peer(k), region(None, None, 0, place))], recv_z.at[k - 1, pl.ds(j0, nj)],
+                      rz_s.at[n], rz_r.at[n], dev(s, peer(k), d)).start()
+            held = recv_z.at[:, pl.ds(j0, nj)]
+            sends.append((rcopy(held, held, rz_s.at[n], rz_r.at[n], sibling), None, n))
+
+        def z_take_pieces(n):
+            b, (j0, nj) = ggroups[n]
             received(recv_z.at[:, pl.ds(j0, nj)], rz_r.at[n])
-            total = z_part(b, group, final, m)[...].astype(F32)
+            total = big[shard_part(n, m, region(None, None, 0, place))].astype(F32)
             for k in range(1, mp):
                 total = total + recv_z[k - 1, pl.ds(j0, nj)].astype(F32)
-            if n + per_grad not in z_first:
-                for k in range(1, mp):
+                if n + per_grad not in z_first:
                     give_credit(n, levels + k, dev(s, peer(mp - k), d))
             piece[b, pl.ds(j0, nj)] = total.astype(BF)
+            spread(n)
+
+        def keep_piece(n):
+            b, (j0, nj) = ggroups[n]
+            piece[b, pl.ds(j0, nj)] = big[shard_part(n, m, region(None, None, 0, place))]
             spread(n)
 
         def spread(n):
@@ -855,8 +837,7 @@
                 z_first_cross(n, i)
                 yield post("xy", size / 16 / (1 << i), 100)
             z_first_cross(n, levels)
-            piece[b, pl.ds(j0, nj)] = big[shard_part(n, m, region(None, None, 0, place))]
-            spread(n)
+            keep_piece(n)
             post("xy", size / 2 / dp / mp * dp / 2, 100)
 
         def across(o):
@@ -878,16 +859,17 @@
                 x_exchange(n, i)
                 yield post("xy", size / 4 / (1 << i), 100)
             x_exchange(n, levels)
+            z_send_pieces(n)
             yield post("z", 2 * size / 2 / dp, 100)
-            finish(n)
+            z_take_pieces(n)
             post("xy", size / 2 / dp / mp * dp / 2, 100)
 
         first, second = range(per_block), range(per_block, 2 * per_block)
         for copy in loads:
             copy.wait()
-        gbuf[0] = jnp.zeros((2, 8, width), F32)
+        gbuf[0] = jnp.zeros((8, width), F32)
         received(gains.at[1 - s, 0], gn_r.at[0])
-        received(gains.at[1 - s, 1], gn_r.at[levels + mp])
+        received(gains.at[1 - s, 1], gn_r.at[1])
         work(2.5, first_norm, 0)
         stage_edges(xext)
         arrived = halo_send(0)
@@ -978,29 +960,36 @@
             launch((1, per_grad + 2 + g), reduce_chain(per_grad + 2 + g))
         halo_wait(2, 0, arrived)
         work(0.5, fill_edges, gpad)
-        work(5.0, in_grad, 0)
+        for half in range(width // COLS):
+            work(2.5, in_grad, 0, None, half)
         for batch in range(batches):
             work(1.0, in_back, 0, batch)
         send_home(x0, ing, 0, 2)
 
         def gain_chain():
-            begin(rcopy(gbuf.at[0], grecv.at[0], gn_s.at[1], gn_r.at[1], sibling))
-            for i in range(levels + 1):
-                yield clock["now"] + LATENCY
-                received(grecv.at[i], gn_r.at[1 + i])
-                gbuf[i + 1] = gbuf[i] + grecv[i]
-                if i < levels:
-                    begin(rcopy(gbuf.at[i + 1], grecv.at[i + 1], gn_s.at[2 + i], gn_r.at[2 + i], partner(i)))
+            own = 2 * d + s
+            grecv[own] = gbuf[0]
+            for o in range(dp):
+                for ss in range(2):
+                    if o or ss:
+                        rcopy(gbuf.at[0], grecv.at[own], gn_s.at[2], gn_r.at[2],
+                              dev(s + ss - 2 * s * ss, m, across(o))).start()
+            held = grecv.at[pl.ds(0, 2 * dp - 1)]
+            sends.append((rcopy(held, held, gn_s.at[2], gn_r.at[2], sibling), None, "gains"))
+            yield clock["now"] + 2 * LATENCY
+            received(held, gn_r.at[2])
+            total = grecv[0]
+            for i in range(1, 2 * dp):
+                total = total + grecv[i]
+            gbuf[1] = total
             for k in range(1, mp):
-                at = levels + k
-                begin(rcopy(gbuf.at[levels + 1], grecv.at[at], gn_s.at[1 + at], gn_r.at[1 + at], dev(s, peer(k), d)))
+                rcopy(gbuf.at[1], gz.at[k - 1], gn_s.at[3], gn_r.at[3], dev(s, peer(k), d)).start()
+            sends.append((rcopy(gz, gz, gn_s.at[3], gn_r.at[3], sibling), None, "gains"))
             yield clock["now"] + 2 * LATENCY
-            total = gbuf[levels + 1]
+            received(gz, gn_r.at[3])
             for k in range(1, mp):
-                at = levels + k
-                received(grecv.at[at], gn_r.at[1 + at])
-                total = total + grecv[at]
-            gbuf[levels + 2] = total
+                total = total + gz[k - 1]
+            gbuf[2] = total
 
         launch((2, 0), gain_chain())
         for n in range(nwg):
@@ -1012,7 +1001,7 @@
                 flush(n)
         complete(list(chains))
         out = pltpu.make_async_copy(
-            gbuf.at[levels + 2, s, :, pl.ds(pl.multiple_of(m * group_rows, group_rows), group_rows)], gout_sum, loc.at[0])
+            gbuf.at[2, :, pl.ds(pl.multiple_of(m * group_rows, group_rows), group_rows)], gout_sum, loc.at[0])
         out.start()
         received(fin, rf_r.at[0])
         flush()
@@ -1066,8 +1055,9 @@
         vm((2 * HALF, q_count + 16, width), F32),
         vm((2, nw, 8, width), F32),
         vm((2, nw, 8, width), F32),
-        vm((levels + 3, 2, 8, width), F32),
-        vm((levels + mp, 2, 8, width), F32),
+        vm((3, 8, width), F32),
+        vm((2 * dp, 8, width), F32),
+        vm((mp - 1, 8, width), F32),
     ] + [vm(recv_shape(i), BF) for i in range(levels)] + [
         dma((per_block, mp - 1, 2)), dma((nwg, mp - 1)), dma((nwg,)),
         dma((nwg, levels)), dma((nwg, levels)),
@@ -1078,7 +1068,7 @@
         dma((ngg,)), dma((ngg,)),
         dma((1 + len(z_first), 3)), dma((1 + len(z_first), 3)),
         dma((ngg, dp)), dma((1,)),
-        dma((1 + levels + mp + 1,)), dma((1 + levels + mp + 1,)),
+        dma((4,)), dma((4,)),
         dma((4, batches, 2)), dma((4, batches, 2)),
         dma((4,)), dma((4,)),
         dma((8,)),
@@ -1129,10 +1119,11 @@
         parts = [(0, KERNEL), (KERNEL, mp), (KERNEL + mp, mp)]
         reads = [pltpu.make_async_copy(fin_in.at[pl.ds(a, n)], held.at[pl.ds(a, n)], sem.at[2 + i])
                  for i, (a, n) in enumerate(parts)]
-        for copy in moves + reads:
+        for copy in reads[:1] + moves + reads[1:]:
             copy.start()
-        one_out[...] = sums_in[0:1, :]
-        two_out[...] = sums_in[1:2, :]
+        first = lax.axis_index("section") == 0
+        one_out[...] = jnp.where(first, sums_in[0:1, :], sums_in[2:3, :])
+        two_out[...] = jnp.where(first, sums_in[1:2, :], sums_in[3:4, :])
         writes = []
 
         def store(src, dst, at):
@@ -1140,17 +1131,17 @@
             copy.start()
             writes.append(copy)
 
-        for i, out in enumerate((blk_out, ing_out)):
-            moves[i].wait()
-            store(acts.at[i], out.at[0], 10 + i)
         reads[0].wait()
         for k in range(KERNEL):
-            conv[k] = held[k].astype(F32).T
+            conv[k] = held[k].T.astype(F32)
             if k % 3 == 2:
                 store(conv.at[pl.ds(k - 2, 3)], conv_out.at[0, pl.ds(k - 2, 3)], 5 + k // 3)
+            if k < 2:
+                moves[k].wait()
+                store(acts.at[k], (blk_out, ing_out)[k].at[0], 10 + k)
         reads[2].wait()
         for j in range(mp):
-            down[:, j * rows:(j + 1) * rows] = held[KERNEL + mp + j].astype(F32).T
+            down[:, j * rows:(j + 1) * rows] = held[KERNEL + mp + j].T.astype(F32)
         store(down, down_out.at[0], 8)
         reads[1].wait()
         for j in range(mp):

time: 213 us -> 211 us (level)
  no operation moved by 1% of the time
where the time goes in v2:
time: 211 us
  Pallas kernels  210 us (100%)
    pallas_call x1, Pallas kernels, per_device(): pl.pallas_call(body, out_shape=(jax.ShapeDtypeStruct(tokens.shape, BF), j...  204 us
    pallas_call x1, Pallas kernels, finalize(): pl.pallas_call(body, out_shape=(jax.ShapeDtypeStruct((1,) + blk.shape, BF...  6.14 us

profile of v2, /device:TPU:0, one launch (start us, length us, event | category | flops | bytes accessed | tf_op | source)
XLA Modules:
  0.0 211.3 jit_solution(3718006265350870127)
XLA Ops:
  0.6 204.3 %shard_map.135 = (bf16[12,128,512]{2,1,0:T(8,128)(2,1)}, bf16[12,128,512]{2,1,0:T(8,128)(2,1)}, bf16[17,128,512]{2,1,0:T(8,128)(2,1)}, f32[8,128]{1,0:T(8,128)},...) custom-call(bf16[12,128,512]{2,1,0:T(8,128)(2,1)} %tok.1, bf16[12,128,512]{2,1,0:T(8,128)(2,1)} %cot.1, s32[12]{0:T(128)} %valid.1, ...), custom_call_target="tpu_custom_call" | custom-call | tf_op jit(solution)/shard_map/pallas_call | solution.py:1092
  204.9 6.1 %shard_map.136 = (bf16[1,12,128,512]{3,2,1,0:T(8,128)(2,1)}, bf16[1,12,128,512]{3,2,1,0:T(8,128)(2,1)}, f32[1,9,512,128]{3,2,1,0:T(8,128)}, f32[1,128]{1,0:T(1,1...) custom-call(bf16[12,128,512]{2,1,0:T(8,128)(2,1)} %get-tuple-element.11.blk_in, ...), custom_call_target="tpu_custom_call" | custom-call | tf_op jit(solution)/shard_map/pallas_call | solution.py:1156
